TPU v7x, 32 devices: a whole 2x2x4 slice. The times are simulated.
32 devices in a mesh: head: 4 (over x, core), blk: 8 (over z, y).
Axes of the slice: x: 2, y: 2, z: 4, core: 2. Of those that a mesh axis runs over, the one named last changes fastest.
Arguments:
- layer_in: bfloat16 [4096, 2048], P(('head', 'blk')), may hold values from -6 to 6
- out_grad: bfloat16 [4096, 2048], P(('head', 'blk')), may hold values from -6 to 6
- norm_gain: bfloat16 [2048], P(('head', 'blk')), may hold values from 0.25 to 1.75
- norm_bias: bfloat16 [2048], P(('head', 'blk')), may hold values from -1.796875 to 1.796875
- w_qkv: bfloat16 [3, 2048, 2048], P(None, ('head', 'blk')), may hold values from -0.125 to 0.125
- b_qkv: bfloat16 [3, 2048], P(None, ('head', 'blk')), may hold values from -0.29882812 to 0.29882812
- w_out: bfloat16 [2048, 2048], P(('head', 'blk')), may hold values from -4 to 4
- b_out: bfloat16 [2048], P(('head', 'blk')), may hold values from -1.796875 to 1.796875
- w_up: bfloat16 [8192, 2048], P(('head', 'blk')), may hold values from -0.125 to 0.125
- b_up: bfloat16 [8192], P(('head', 'blk')), may hold values from -1.796875 to 1.796875
- w_down: bfloat16 [8192, 2048], P(('head', 'blk')), may hold values from -0.0625 to 0.0625
- b_down: bfloat16 [2048], P(('head', 'blk')), may hold values from -1.796875 to 1.796875
- seq_lengths: int32 [4], replicated, may hold values from 1 to 2048, 4096 in all
- token_place: int32 [4096], replicated, may hold values from 0 to 4095, as said below
Outputs:
- layer_out: bfloat16 [4096, 2048], P(('head', 'blk'))
- layer_in_grad: bfloat16 [4096, 2048], P(('head', 'blk'))
- norm_gain_grad: float32 [2048], P(('head', 'blk'))
- norm_bias_grad: float32 [2048], P(('head', 'blk'))
- w_qkv_grad: float32 [3, 2048, 2048], P(None, ('head', 'blk'))
- b_qkv_grad: float32 [3, 2048], P(None, ('head', 'blk'))
- w_out_grad: float32 [2048, 2048], P(('head', 'blk'))
- b_out_grad: float32 [2048], P(('head', 'blk'))
- w_up_grad: float32 [8192, 2048], P(('head', 'blk'))
- b_up_grad: float32 [8192], P(('head', 'blk'))
- w_down_grad: float32 [8192, 2048], P(('head', 'blk'))
- b_down_grad: float32 [2048], P(('head', 'blk'))
Inputs may be any that keep to these rules, and one draw needn't show every extreme that they name: `seq_lengths`: sequence i fills the packed positions after those of sequences 0 to i - 1; the lengths add up to 4096. A permutation of the packed positions: row r of every row array is packed position token_place[r]. The 128 rows of each device hold one position of each aligned run of 32 packed positions.
All inputs are finite; a program needn't handle non-finite values.
Results may differ from a plain program's by a relative error of at most 0.014.
Values may be sent and summed in bfloat16 or wider, within the bound.
No kernel may reach another device: no remote copies, remote signals or barrier semaphores. Data moves between devices by JAX's collectives and lax.ppermute only.
A program may use at most 512 MiB of HBM per device.

v0:
```python
import jax
import jax.numpy as jnp
from jax import lax
from jax.sharding import PartitionSpec as P

HEAD_DIM = 64
ROT = 32


def passed_along(block, axis, distance):
    devices = range(lax.axis_size(axis))
    route = [((i - distance) % len(devices), i) for i in devices]
    return lax.ppermute(block, axis, route)


def mat_nt(left_op, right_op):
    return lax.dot_general(
        left_op, right_op, (((1,), (1,)), ((), ())), preferred_element_type=jnp.float32
    )


def mat_tn(left_op, right_op):
    return lax.dot_general(
        left_op, right_op, (((0,), (0,)), ((), ())), preferred_element_type=jnp.float32
    )


def seq_meta(packed, lengths):
    starts = jnp.cumsum(lengths) - lengths
    inside = packed[:, None] >= starts[None, :]
    segment = jnp.sum(inside.astype(jnp.int32), axis=1) - 1
    opening = jnp.max(jnp.where(inside, starts[None, :], 0), axis=1)
    return (segment, packed - opening)


def rotate(values, positions, direction):
    row_count = values.shape[0]
    split_heads = values.reshape(row_count, -1, HEAD_DIM)
    half_rot = ROT // 2
    lower_half = split_heads[:, :, :half_rot]
    upper_half = split_heads[:, :, half_rot:ROT]
    frequency = 10000.0 ** (-2.0 * jnp.arange(half_rot, dtype=jnp.float32) / ROT)
    angles = positions.astype(jnp.float32)[:, None] * frequency[None, :]
    cosine = jnp.cos(angles)[:, None, :]
    sine_part = direction * jnp.sin(angles)[:, None, :]
    turned = jnp.concatenate(
        [
            lower_half * cosine - upper_half * sine_part,
            upper_half * cosine + lower_half * sine_part,
            split_heads[:, :, ROT:],
        ],
        axis=2,
    )
    return turned.reshape(row_count, -1)


def normalize(inputs, gain_vec, offset):
    center = jnp.mean(inputs, axis=-1, keepdims=True)
    centered = inputs - center
    variance = jnp.mean(centered * centered, axis=-1, keepdims=True)
    return centered * lax.rsqrt(variance + 1e-05) * gain_vec + offset


def gelu_tanh(values):
    return jax.nn.gelu(values, approximate=True)


def gelu_back(hidden, act_grad):
    _, pullback = jax.vjp(gelu_tanh, hidden)
    return pullback(act_grad)[0]


def rotate_rows(projected, positions):
    return jnp.stack(
        [
            rotate(projected[:, 0], positions, 1.0),
            rotate(projected[:, 1], positions, 1.0),
            projected[:, 2],
        ],
        axis=1,
    ).astype(jnp.bfloat16)


def attention_forward(qkv_heads, key_order, seq_lengths, query_idx):
    query_rows = qkv_heads.shape[0]
    width = qkv_heads.shape[2]
    head_count = width // HEAD_DIM
    scaling = HEAD_DIM ** (-0.5)
    queries = qkv_heads[:, 0].reshape(query_rows, head_count, HEAD_DIM)
    query_seg, _ = seq_meta(query_idx, seq_lengths)
    initial = (
        jnp.full((head_count, query_rows), -1e30, jnp.float32),
        jnp.zeros((head_count, query_rows), jnp.float32),
        jnp.zeros((query_rows, width), jnp.float32),
    )
    kv_piece = lax.all_gather(qkv_heads[:, 1:], "blk", axis=0, tiled=True)
    block_count = kv_piece.shape[0] // query_rows

    def one_block(block_num, block_state):
        run_max, run_sum, accum = block_state
        start = block_num * query_rows
        kv_block = lax.dynamic_slice_in_dim(kv_piece, start, query_rows, 0)
        key_idx = lax.dynamic_slice_in_dim(key_order, start, query_rows, 0)
        key_seg, _ = seq_meta(key_idx, seq_lengths)
        visible = (
            (query_seg[:, None] == key_seg[None, :]) & (key_idx[None, :] <= query_idx[:, None])
        )[None]
        key_heads = kv_block[:, 0].reshape(query_rows, head_count, HEAD_DIM)
        value_heads = kv_block[:, 1].reshape(query_rows, head_count, HEAD_DIM)
        scores = (
            jnp.einsum("qhd,khd->hqk", queries, key_heads, preferred_element_type=jnp.float32)
            * scaling
        )
        new_max = jnp.maximum(run_max, jnp.max(jnp.where(visible, scores, -1e30), axis=2))
        weights = jnp.where(visible, jnp.exp(scores - new_max[:, :, None]), 0.0)
        rescale = jnp.exp(run_max - new_max)
        new_sum = run_sum * rescale + jnp.sum(weights, axis=2)
        mixed = jnp.einsum(
            "hqk,khd->qhd",
            weights.astype(jnp.bfloat16),
            value_heads,
            preferred_element_type=jnp.float32,
        )
        updated = accum.reshape(query_rows, head_count, HEAD_DIM) * rescale.T[:, :, None] + mixed
        return (new_max, new_sum, updated.reshape(query_rows, width))

    run_max, run_sum, accum = lax.fori_loop(0, block_count, one_block, initial)
    attended = accum / jnp.repeat(run_sum.T, HEAD_DIM, axis=1)
    return (attended, run_max + jnp.log(run_sum))


def attention_backward(
    qkv_heads, attended, attended_grad, log_total, key_order, seq_lengths, query_idx, positions
):
    query_rows = qkv_heads.shape[0]
    width = qkv_heads.shape[2]
    head_count = width // HEAD_DIM
    scaling = HEAD_DIM ** (-0.5)
    cycle_size = lax.axis_size("blk")
    cycle_index = lax.axis_index("blk")
    queries = qkv_heads[:, 0].reshape(query_rows, head_count, HEAD_DIM)
    grad_heads = attended_grad.reshape(query_rows, head_count, HEAD_DIM)
    query_seg, _ = seq_meta(query_idx, seq_lengths)
    deltas = jnp.sum(
        (attended_grad.astype(jnp.float32) * attended).reshape(query_rows, head_count, HEAD_DIM),
        axis=2,
    ).T

    def one_turn(cycle_turn, cycle_state):
        kv_block, kv_grad, query_grad = cycle_state
        source = (cycle_index - cycle_turn) % cycle_size
        key_idx = lax.dynamic_slice_in_dim(key_order, source * query_rows, query_rows, 0)
        key_seg, _ = seq_meta(key_idx, seq_lengths)
        visible = (
            (query_seg[:, None] == key_seg[None, :]) & (key_idx[None, :] <= query_idx[:, None])
        )[None]
        key_heads = kv_block[:, 0].reshape(query_rows, head_count, HEAD_DIM)
        value_heads = kv_block[:, 1].reshape(query_rows, head_count, HEAD_DIM)
        scores = (
            jnp.einsum("qhd,khd->hqk", queries, key_heads, preferred_element_type=jnp.float32)
            * scaling
        )
        probs = jnp.where(visible, jnp.exp(scores - log_total[:, :, None]), 0.0)
        value_part = jnp.einsum(
            "hqk,qhd->khd",
            probs.astype(jnp.bfloat16),
            grad_heads,
            preferred_element_type=jnp.float32,
        )
        prob_grad = jnp.einsum(
            "qhd,khd->hqk", grad_heads, value_heads, preferred_element_type=jnp.float32
        )
        score_grad = (probs * (prob_grad - deltas[:, :, None])).astype(jnp.bfloat16)
        query_part = (
            jnp.einsum("hqk,khd->qhd", score_grad, key_heads, preferred_element_type=jnp.float32)
            * scaling
        )
        key_part = (
            jnp.einsum("hqk,qhd->khd", score_grad, queries, preferred_element_type=jnp.float32)
            * scaling
        )
        kv_grad = kv_grad + jnp.stack(
            [key_part.reshape(query_rows, width), value_part.reshape(query_rows, width)], axis=1
        )
        query_grad = query_grad + query_part.reshape(query_rows, width)
        kv_grad = passed_along(kv_grad.astype(jnp.bfloat16), "blk", 1).astype(kv_grad.dtype)
        kv_block = passed_along(kv_block, "blk", 1)
        return (kv_block, kv_grad, query_grad)

    initial = (
        qkv_heads[:, 1:],
        jnp.zeros((query_rows, 2, width), jnp.float32),
        jnp.zeros((query_rows, width), jnp.float32),
    )
    _, kv_grad, query_grad = lax.fori_loop(0, cycle_size, one_turn, initial)
    return jnp.stack(
        [
            rotate(query_grad, positions, -1.0),
            rotate(kv_grad[:, 0], positions, -1.0),
            kv_grad[:, 1],
        ],
        axis=1,
    ).astype(jnp.bfloat16)


def per_device(
    layer_in,
    out_grad,
    norm_gain,
    norm_bias,
    w_qkv,
    b_qkv,
    w_out,
    b_out,
    w_up,
    b_up,
    w_down,
    b_down,
    seq_lengths,
    token_place,
):
    group_size = lax.axis_size("head")
    cycle_size = lax.axis_size("blk")
    group_index = lax.axis_index("head")
    cycle_index = lax.axis_index("blk")
    tok_rows = layer_in.shape[0]
    place_grid = token_place.reshape(group_size, cycle_size, tok_rows)
    own_idx = lax.dynamic_slice_in_dim(
        token_place, (group_index * cycle_size + cycle_index) * tok_rows, tok_rows, 0
    )
    group_idx = lax.dynamic_slice_in_dim(place_grid, cycle_index, 1, 1).reshape(-1)
    key_order = jnp.transpose(place_grid, (1, 0, 2)).reshape(-1)
    _, group_pos = seq_meta(group_idx, seq_lengths)
    inputs = layer_in.astype(jnp.float32)
    grad_out = out_grad.astype(jnp.float32)
    bias_grad = jnp.sum(grad_out, axis=0)
    (
        gain_all,
        offset_all,
        wqkv_all,
        bqkv_all,
        wout_all,
        bout_all,
        wup_all,
        bup_all,
        wdown_all,
        bdown_all,
    ) = (
        lax.all_gather(norm_gain, ("head", "blk"), axis=0, tiled=True),
        lax.all_gather(norm_bias, ("head", "blk"), axis=0, tiled=True),
        lax.all_gather(w_qkv, ("head", "blk"), axis=1, tiled=True),
        lax.all_gather(b_qkv, ("head", "blk"), axis=1, tiled=True),
        lax.all_gather(w_out, ("head", "blk"), axis=0, tiled=True),
        lax.all_gather(b_out, ("head", "blk"), axis=0, tiled=True),
        lax.all_gather(w_up, ("head", "blk"), axis=0, tiled=True),
        lax.all_gather(b_up, ("head", "blk"), axis=0, tiled=True),
        lax.all_gather(w_down, ("head", "blk"), axis=0, tiled=True),
        lax.all_gather(b_down, ("head", "blk"), axis=0, tiled=True),
    )
    gain_f = gain_all.astype(jnp.float32)
    offset_f = offset_all.astype(jnp.float32)
    normed_low = normalize(inputs, gain_f, offset_f).astype(jnp.bfloat16)
    projected = (
        jnp.einsum("ti,wci->twc", normed_low, wqkv_all, preferred_element_type=jnp.float32)
        + bqkv_all.astype(jnp.float32)[None]
    )
    _, own_pos = seq_meta(own_idx, seq_lengths)
    qkv_heads = lax.all_to_all(
        rotate_rows(projected, own_pos), "head", split_axis=2, concat_axis=0, tiled=True
    )
    attended, log_total = attention_forward(qkv_heads, key_order, seq_lengths, group_idx)
    attended_low = lax.all_to_all(
        attended.astype(jnp.bfloat16), "head", split_axis=0, concat_axis=1, tiled=True
    )
    hidden = mat_nt(normed_low, wup_all) + bup_all.astype(jnp.float32)
    active = gelu_tanh(hidden).astype(jnp.bfloat16)
    mixed = (
        inputs
        + jnp.dot(attended_low, wout_all, preferred_element_type=jnp.float32)
        + bout_all.astype(jnp.float32)
    )
    mixed = (
        mixed
        + jnp.dot(active, wdown_all, preferred_element_type=jnp.float32)
        + bdown_all.astype(jnp.float32)
    )
    layer_out = mixed.astype(jnp.bfloat16)
    wqkv_back, wout_back, wup_back, wdown_back = (
        lax.all_gather(w_qkv, ("head", "blk"), axis=1, tiled=True),
        lax.all_gather(w_out, ("head", "blk"), axis=0, tiled=True),
        lax.all_gather(w_up, ("head", "blk"), axis=0, tiled=True),
        lax.all_gather(w_down, ("head", "blk"), axis=0, tiled=True),
    )
    w_down_g = mat_tn(active, out_grad)
    hidden_grad = gelu_back(hidden, mat_nt(out_grad, wdown_back)).astype(jnp.bfloat16)
    w_up_g = mat_tn(hidden_grad, normed_low)
    b_up_g = jnp.sum(hidden_grad.astype(jnp.float32), axis=0)
    w_up_o, b_up_o, w_down_o, bias_o = (
        lax.psum_scatter(w_up_g, ("head", "blk"), scatter_dimension=0, tiled=True),
        lax.psum_scatter(b_up_g, ("head", "blk"), scatter_dimension=0, tiled=True),
        lax.psum_scatter(w_down_g, ("head", "blk"), scatter_dimension=0, tiled=True),
        lax.psum_scatter(bias_grad, ("head", "blk"), scatter_dimension=0, tiled=True),
    )
    normed_grad = jnp.dot(hidden_grad, wup_back, preferred_element_type=jnp.float32)
    w_out_g = mat_tn(attended_low, out_grad)
    heads_grad = lax.all_to_all(
        mat_nt(out_grad, wout_back).astype(jnp.bfloat16),
        "head",
        split_axis=1,
        concat_axis=0,
        tiled=True,
    )
    qkv_grad = attention_backward(
        qkv_heads, attended, heads_grad, log_total, key_order, seq_lengths, group_idx, group_pos
    )
    rows_grad = lax.all_to_all(qkv_grad, "head", split_axis=0, concat_axis=2, tiled=True)
    w_qkv_g = jnp.einsum("twc,ti->wci", rows_grad, normed_low, preferred_element_type=jnp.float32)
    b_qkv_g = jnp.sum(rows_grad.astype(jnp.float32), axis=0)
    normed_grad = normed_grad + jnp.einsum(
        "twc,wci->ti", rows_grad, wqkv_back, preferred_element_type=jnp.float32
    )
    _, norm_pull = jax.vjp(normalize, inputs, gain_f, offset_f)
    input_part, gain_g, offset_g = norm_pull(normed_grad)
    w_qkv_o, b_qkv_o, w_out_o, gain_o, offset_o = (
        lax.psum_scatter(w_qkv_g, ("head", "blk"), scatter_dimension=1, tiled=True),
        lax.psum_scatter(b_qkv_g, ("head", "blk"), scatter_dimension=1, tiled=True),
        lax.psum_scatter(w_out_g, ("head", "blk"), scatter_dimension=0, tiled=True),
        lax.psum_scatter(gain_g, ("head", "blk"), scatter_dimension=0, tiled=True),
        lax.psum_scatter(offset_g, ("head", "blk"), scatter_dimension=0, tiled=True),
    )
    input_grad = (grad_out + input_part).astype(jnp.bfloat16)
    return (
        layer_out,
        input_grad,
        gain_o,
        offset_o,
        w_qkv_o,
        b_qkv_o,
        w_out_o,
        bias_o,
        w_up_o,
        b_up_o,
        w_down_o,
        bias_o,
    )


def solution(mesh):
    in_specs = (
        P(("head", "blk"), None),
        P(("head", "blk"), None),
        P(("head", "blk")),
        P(("head", "blk")),
        P(None, ("head", "blk"), None),
        P(None, ("head", "blk")),
        P(("head", "blk"), None),
        P(("head", "blk")),
        P(("head", "blk"), None),
        P(("head", "blk")),
        P(("head", "blk"), None),
        P(("head", "blk")),
        P(),
        P(),
    )
    out_specs = (
        P(("head", "blk"), None),
        P(("head", "blk"), None),
        P(("head", "blk")),
        P(("head", "blk")),
        P(None, ("head", "blk"), None),
        P(None, ("head", "blk")),
        P(("head", "blk"), None),
        P(("head", "blk")),
        P(("head", "blk"), None),
        P(("head", "blk")),
        P(("head", "blk"), None),
        P(("head", "blk")),
    )
    return jax.shard_map(
        per_device, mesh=mesh, in_specs=in_specs, out_specs=out_specs, check_vma=False
    )
```

profile of v0, /device:TPU:0, one launch (start us, length us, event | category | flops | bytes accessed | tf_op | source)
XLA Modules:
  0.0 5576.3 jit_solution(10923374492784210566)
XLA Ops:
  8.7 70.7 %all-gather = bf16[32,64,3]{1,2,0:T(4,128)(2,1)S(1)} all-gather(bf16[1,64,3]{1,2,0:T(4,128)(2,1)} %bitcast.254), channel_id=1, replica_groups=mesh['head'=4,'blk'=8] {'head','blk'}, dimensions={0}, use_global_device_ids=true | all-gather | bytes 12672 | tf_op jit(solution)/shard_map/all_gather | solution.py:252
  82.9 42.0 all-reduce.9
  131.2 37.9 all-gather.8.cloned.1.call-done
  195.5 34.9 all_to_all.71
  279.6 104.1 %all-gather.10.cloned.1.call-done = bf16[4096,2,512]{0,2,1:T(8,128)(2,1)} async-done(((bf16[512,2,512]{0,2,1:T(8,128)(2,1)}), bf16[4096,2,512]{0,2,1:T(8,128)(2,1)}) %all-gather.10.cloned.1.call-update) | async-done | bytes 8388624 | tf_op jit(solution)/shard_map/all_gather | solution.py:96
  384.8 133.2 %while.40 = (s32[]{:T(128)}, f32[8,512]{1,0:T(8,128)S(1)}, f32[8,512]{1,0:T(8,128)S(1)}, f32[512,512]{0,1:T(8,128)}, s32[512]{0:T(512)S(1)}, /*index=5*/s32[4096...) while((s32[]{:T(128)}, f32[8,512]{1,0:T(8,128)S(1)}, ...), condition=%wide.region_9.10_spmd.clone, body=%wide.region_5.9_spmd.clone.sunk | while | flops 561281024 | bytes 65818896 | solution.py:127
  521.9 635.7 %while.41 = (s32[]{:T(128)}, bf16[512,2,512]{0,2,1:T(8,128)(2,1)S(1)}, f32[512,2,512]{0,2,1:T(8,128)}, f32[512,512]{0,1:T(8,128)}, s32[512]{0:T(512)S(1)}, /*ind...) while((s32[]{:T(128)}, ...), condition=%wide.region_13.14_spmd.clone, body=%wide.region_11.13_spmd.clone.sunk | while | flops 1367611392 | bytes 105189960 | solution.py:195
  539.7 43.4 collective-permute-done.1
  585.9 34.2 collective-permute-done
  636.3 41.7 collective-permute-done.1
  680.9 38.8 collective-permute-done
  735.6 32.7 collective-permute-done.1
  809.8 53.2 collective-permute-done.1
  865.9 39.7 collective-permute-done
  921.6 35.8 collective-permute-done.1
  1114.6 25.1 collective-permute-done.1
  1179.5 25.4 all-to-all-done.3
  1242.5 63.6 %all-gather.1 = bf16[32,1,256]{2,1,0:T(2,128)(2,1)S(1)} all-gather(bf16[1,1,256]{2,1,0:T(2,128)(2,1)S(1)} %reshape.477), channel_id=1, replica_groups=mesh['head'=4,'blk'=8] {'head','blk'}, dimensions={0}, use_global_device_ids=true | all-gather | bytes 16896 | tf_op jit(solution)/shard_map/all_gather | solution.py:256
  1369.6 25.9 fusion.58
  1450.5 45.8 all-reduce.8
  1499.5 201.2 %reduce-scatter.10.cloned.1.call-done = f32[64,2048]{1,0:T(8,128)} async-done(((f32[2048,2048]{1,0:T(8,128)}), f32[64,2048]{1,0:T(8,128)}) %reduce-scatter.10.cloned.1.call-update) | async-done | bytes 524304 | tf_op jit(solution)/shard_map/reduce_scatter | solution.py:327
  1700.7 1056.7 %reduce-scatter.8.cloned.1.call-done = f32[3,64,2048]{2,1,0:T(8,128)} async-done(((f32[3,2048,2048]{2,1,0:T(8,128)}), f32[3,64,2048]{2,1,0:T(8,128)}) %reduce-scatter.8.cloned.1.call-update) | async-done | bytes 1572880 | tf_op jit(solution)/shard_map/reduce_scatter | solution.py:325
  2757.5 1405.6 %reduce-scatter.12.cloned.1.call-done = f32[256,2048]{1,0:T(8,128)} async-done(((f32[8192,2048]{1,0:T(8,128)}), f32[256,2048]{1,0:T(8,128)}) %reduce-scatter.12.cloned.1.call-update) | async-done | bytes 2097168 | tf_op jit(solution)/shard_map/reduce_scatter | solution.py:299
  4163.0 1405.4 %reduce-scatter.14.cloned.1.call-done = f32[256,2048]{1,0:T(8,128)} async-done(((f32[8192,2048]{1,0:T(8,128)}), f32[256,2048]{1,0:T(8,128)}) %reduce-scatter.14.cloned.1.call-update) | async-done | bytes 2097168 | tf_op jit(solution)/shard_map/reduce_scatter | solution.py:301
  (493 shorter events, 695.7 us)
Async XLA Ops:
  7.2 162.0 %all-gather.8.cloned.1.call-start = ((), (), s32[]{:S(2)}) async-start(), calls=%async_computation.9 | async-start | bytes 25952256 | tf_op jit(solution)/shard_map/all_gather | solution.py:251
  7.9 249.2 %all-gather.12.cloned.1.call-start = ((), (), s32[]{:S(2)}) async-start(), calls=%async_computation.11 | async-start | bytes 8650752 | tf_op jit(solution)/shard_map/all_gather | solution.py:253
  8.7 375.0 %all-gather.10.cloned.1.call-start = ((), (), s32[]{:S(2)}) async-start(), calls=%async_computation.10 | async-start | bytes 9437184 | tf_op jit(solution)/shard_map/all_gather | solution.py:96
  236.7 1069.5 %all-gather.16.cloned.1.call-start = ((), (), s32[]{:S(2)}) async-start(), calls=%async_computation.13 | async-start | bytes 34603008 | tf_op jit(solution)/shard_map/all_gather | solution.py:257
  237.2 1086.4 %all-gather.14.cloned.1.call-start = ((), (), s32[]{:S(2)}) async-start(), calls=%async_computation.12 | async-start | bytes 34603008 | tf_op jit(solution)/shard_map/all_gather | solution.py:255
  534.1 48.9 collective-permute-start.1
  535.7 84.4 %collective-permute-start = (bf16[512,2,512]{0,2,1:T(8,128)(2,1)S(1)}, bf16[512,2,512]{0,2,1:T(8,128)(2,1)S(1)}, u32[]{:S(2)}, u32[]{:S(2)}) collective-permute-start(bf16[512,2,512]{0,2,1:T(8,128)(2,1)S(1)} %copy.180), channel_id=1, source_target_pairs={{7,0},{0,1},{1,2},{2,3},{3,4},{4,5},{5,6},{6,7},{15,8},{8,9},{9,10... | collective-permute-start | bytes 3145736 | tf_op jit(solution)/shard_map/while/body/eval_jaxpr/ppermute | solution.py:13
  632.1 45.9 collective-permute-start.1
  632.1 87.6 %collective-permute-start = (bf16[512,2,512]{0,2,1:T(8,128)(2,1)S(1)}, bf16[512,2,512]{0,2,1:T(8,128)(2,1)S(1)}, u32[]{:S(2)}, u32[]{:S(2)}) collective-permute-start(bf16[512,2,512]{0,2,1:T(8,128)(2,1)S(1)} %copy.180), channel_id=1, source_target_pairs={{7,0},{0,1},{1,2},{2,3},{3,4},{4,5},{5,6},{6,7},{15,8},{8,9},{9,10... | collective-permute-start | bytes 3145736 | tf_op jit(solution)/shard_map/while/body/eval_jaxpr/ppermute | solution.py:13
  731.6 36.7 collective-permute-start.1
  731.6 58.4 %collective-permute-start = (bf16[512,2,512]{0,2,1:T(8,128)(2,1)S(1)}, bf16[512,2,512]{0,2,1:T(8,128)(2,1)S(1)}, u32[]{:S(2)}, u32[]{:S(2)}) collective-permute-start(bf16[512,2,512]{0,2,1:T(8,128)(2,1)S(1)} %copy.180), channel_id=1, source_target_pairs={{7,0},{0,1},{1,2},{2,3},{3,4},{4,5},{5,6},{6,7},{15,8},{8,9},{9,10... | collective-permute-start | bytes 3145736 | tf_op jit(solution)/shard_map/while/body/eval_jaxpr/ppermute | solution.py:13
  801.9 61.2 %collective-permute-start.1 = (bf16[512,2,512]{0,2,1:T(8,128)(2,1)}, bf16[512,2,512]{0,2,1:T(8,128)(2,1)}, u32[]{:S(2)}, u32[]{:S(2)}) collective-permute-start(bf16[512,2,512]{0,2,1:T(8,128)(2,1)} %fusion.147), channel_id=1, source_target_pairs={{7,0},{0,1},{1,2},{2,3},{3,4},{4,5},{5,6},{6,7},{15,8},{8,9},{9,10... | collective-permute-start | bytes 3145736 | tf_op jit(solution)/shard_map/while/body/eval_jaxpr/ppermute | solution.py:13
  801.9 103.7 %collective-permute-start = (bf16[512,2,512]{0,2,1:T(8,128)(2,1)S(1)}, bf16[512,2,512]{0,2,1:T(8,128)(2,1)S(1)}, u32[]{:S(2)}, u32[]{:S(2)}) collective-permute-start(bf16[512,2,512]{0,2,1:T(8,128)(2,1)S(1)} %copy.180), channel_id=1, source_target_pairs={{7,0},{0,1},{1,2},{2,3},{3,4},{4,5},{5,6},{6,7},{15,8},{8,9},{9,10... | collective-permute-start | bytes 3145736 | tf_op jit(solution)/shard_map/while/body/eval_jaxpr/ppermute | solution.py:13
  917.5 40.0 collective-permute-start.1
  917.5 60.6 %collective-permute-start = (bf16[512,2,512]{0,2,1:T(8,128)(2,1)S(1)}, bf16[512,2,512]{0,2,1:T(8,128)(2,1)S(1)}, u32[]{:S(2)}, u32[]{:S(2)}) collective-permute-start(bf16[512,2,512]{0,2,1:T(8,128)(2,1)S(1)} %copy.180), channel_id=1, source_target_pairs={{7,0},{0,1},{1,2},{2,3},{3,4},{4,5},{5,6},{6,7},{15,8},{8,9},{9,10... | collective-permute-start | bytes 3145736 | tf_op jit(solution)/shard_map/while/body/eval_jaxpr/ppermute | solution.py:13
  990.0 48.8 collective-permute-start
  1050.8 47.9 collective-permute-start
  1110.6 47.0 collective-permute-start
  1174.6 30.3 all-to-all-start.3
  1179.1 319.0 %reduce-scatter.16.cloned.1.call-start = ((), (), s32[]{:S(2)}) async-start(), calls=%async_computation.18 | async-start | bytes 1081344
  1210.5 490.2 %reduce-scatter.10.cloned.1.call-start = ((), (), s32[]{:S(2)}) async-start(), calls=%async_computation.15 | async-start | bytes 17301504 | tf_op jit(solution)/shard_map/reduce_scatter | solution.py:327
  1219.2 1538.3 %reduce-scatter.8.cloned.1.call-start = ((), (), s32[]{:S(2)}) async-start(), calls=%async_computation.14 | async-start | bytes 51904512 | tf_op jit(solution)/shard_map/reduce_scatter | solution.py:325
  1241.9 2921.2 %reduce-scatter.12.cloned.1.call-start = ((), (), s32[]{:S(2)}) async-start(), calls=%async_computation.16 | async-start | bytes 69206016 | tf_op jit(solution)/shard_map/reduce_scatter | solution.py:299
  1369.6 4198.9 %reduce-scatter.14.cloned.1.call-start = ((), (), s32[]{:S(2)}) async-start(), calls=%async_computation.17 | async-start | bytes 69206016 | tf_op jit(solution)/shard_map/reduce_scatter | solution.py:301
  (77 other events, 5365.0 us)
Sparse Core Ops, SparseCore 0:
  11.1 158.0 all-gather.7
  172.2 84.9 all-gather.11
  259.8 123.8 all-gather.9
  386.5 195.8 all-gather.15
  585.2 349.9 all-gather.13
  1210.7 131.1 reduce-scatter.15
  1344.8 355.8 reduce-scatter.9
  1703.7 1053.7 reduce-scatter.7
  2760.5 1402.4 reduce-scatter.11
  4165.9 1402.4 reduce-scatter.13
where the time goes:
time: 5590 us; the launch traced here: 5580 us
  waiting for transfers between devices  4750 us (85%)
  matrix products  349 us (6%)
  blocking collectives  257 us (5%)
  other arithmetic  106 us (2%)
  local copies, waits for them, and re-layouts  78.1 us (1%)
    reduce_scatter x1, waiting for transfers between devices, per_device(): lax.psum_scatter(w_up_g, ('head', 'blk'), scatter_dimension=0, tiled=True)  1410 us
    reduce_scatter x1, waiting for transfers between devices, per_device(): lax.psum_scatter(w_down_g, ('head', 'blk'), scatter_dimension=0, tiled=True)  1410 us
    reduce_scatter x1, waiting for transfers between devices, per_device(): lax.psum_scatter(w_qkv_g, ('head', 'blk'), scatter_dimension=1, tiled=True)  1060 us
    ppermute x16, waiting for transfers between devices, passed_along(): return lax.ppermute(block, axis, route)  478 us
    reduce_scatter x1, waiting for transfers between devices, per_device(): lax.psum_scatter(w_out_g, ('head', 'blk'), scatter_dimension=0, tiled=True)  201 us
  transfers between devices with their start and end apart: 29, of which 26 were waited for; matrix products, arithmetic and copies ran while one was open for 9% of the time, Pallas kernels for 0%

commit v1 on v0

v1 whole, which is shorter than its diff:
```python
import jax
import jax.numpy as jnp
from jax import lax
from jax.experimental import pallas as pl
from jax.experimental.pallas import tpu as pltpu
from jax.sharding import PartitionSpec as P

HEAD_DIM = 64
ROT = 32
AXES = ("head", "blk")
GROUP = 16
CHUNK = 512
NEG = -1e30
F32 = jnp.float32
BF16 = jnp.bfloat16


def swap(block, mask, count):
    return lax.ppermute(block, AXES, [(i, i ^ mask) for i in range(count)])


def dot_nn(a, b):
    return lax.dot_general(a, b, (((1,), (0,)), ((), ())), preferred_element_type=F32)


def dot_nt(a, b):
    return lax.dot_general(a, b, (((1,), (1,)), ((), ())), preferred_element_type=F32)


def dot_tn(a, b):
    return lax.dot_general(a, b, (((0,), (0,)), ((), ())), preferred_element_type=F32)


def seq_meta(packed, lengths):
    starts = jnp.cumsum(lengths) - lengths
    inside = packed[..., None] >= starts
    opening = jnp.max(jnp.where(inside, starts, 0), axis=-1)
    return opening, packed - opening


def plan_of(heads, blks):
    core = blks
    others = [1 << i for i in range((heads * blks).bit_length() - 1) if (1 << i) != core]
    if heads * blks == 32:
        y, z1, z2, x = others
        return core, [
            ((0, 48), (z2, z1, y, x)),
            ((48, 96), (z2, x, z1, y)),
            ((96, 128), (z2, y, x, z1)),
        ]
    turned = others[1:] + others[:1]
    return core, [((0, 64), tuple(others)), ((64, 128), tuple(turned))]


def slot_masks(core, order):
    masks = [0]
    for mask in tuple(order) + (core,):
        masks = masks + [m ^ mask for m in masks]
    return masks


def turn_rows(top, low, cosine, sine):
    return top * cosine - low * sine, low * cosine + top * sine


def rope_t(u, cosine, sine):
    half = ROT // 2
    first, second = turn_rows(u[:half], u[half:ROT], cosine, sine)
    return jnp.concatenate([first, second, u[ROT:]], axis=0)


def forward_kernel(
    lo_ref, mid_ref, z_ref, bias_ref, cos_ref, sin_ref, pq_ref, lq_ref, kp_ref,
    att_ref, ot_ref, lse_ref, q_ref, k_ref, v_ref, qt_ref, kt_ref, dvt_ref,
):
    t = pl.program_id(0)
    slots = z_ref.shape[0]
    tile = slots * GROUP
    chunk = q_ref.shape[1]
    per = tile // chunk
    z = z_ref[...].reshape(tile, 3 * HEAD_DIM) + bias_ref[...]
    for c in range(per):
        index = t * per + c
        cosine, sine = cos_ref[c], sin_ref[c]
        zt = z[c * chunk : (c + 1) * chunk].T
        qt = rope_t(zt[:HEAD_DIM], cosine, sine).astype(BF16).astype(F32)
        kt = rope_t(zt[HEAD_DIM : 2 * HEAD_DIM], cosine, sine).astype(BF16).astype(F32)
        vt = zt[2 * HEAD_DIM :].astype(BF16).astype(F32)
        q_ref[index] = qt.T.astype(BF16)
        k_ref[index] = kt.T.astype(BF16)
        v_ref[index] = vt.T.astype(BF16)
        qt_ref[index] = (qt * HEAD_DIM**-0.5).astype(BF16)
        kt_ref[index] = kt.astype(BF16)
        dvt_ref[index] = vt.astype(BF16)
    outs = []
    for c in range(per):
        qt = qt_ref[t * per + c]
        query_pos, query_lo = pq_ref[c], lq_ref[c]

        def step(kc, state, masked):
            run_max, run_sum, acc = state
            scores = dot_nn(k_ref[kc], qt)
            if masked:
                key_pos = kp_ref[kc]
                visible = (key_pos <= query_pos) & (key_pos >= query_lo)
                scores = jnp.where(visible, scores, NEG)
            new_max = jnp.maximum(run_max, jnp.max(scores, axis=0, keepdims=True))
            weights = jnp.exp(scores - new_max)
            if masked:
                weights = jnp.where(visible, weights, 0.0)
            rescale = jnp.exp(run_max - new_max)
            run_sum = run_sum * rescale + jnp.sum(weights, axis=0, keepdims=True)
            acc = acc * rescale + dot_nn(dvt_ref[kc], weights.astype(BF16))
            return new_max, run_sum, acc

        state = (
            jnp.full((1, chunk), NEG, F32),
            jnp.zeros((1, chunk), F32),
            jnp.zeros((HEAD_DIM, chunk), F32),
        )
        state = lax.fori_loop(lo_ref[t], mid_ref[t], lambda i, s: step(i, s, True), state)
        state = lax.fori_loop(mid_ref[t], t * per, lambda i, s: step(i, s, False), state)
        state = lax.fori_loop(t * per, (t + 1) * per, lambda i, s: step(i, s, True), state)
        run_max, run_sum, acc = state
        out = acc / run_sum
        ot_ref[c] = out
        lse_ref[c] = run_max + jnp.log(run_sum)
        outs.append(out.T)
    att = outs[0] if per == 1 else jnp.concatenate(outs, axis=0)
    att_ref[...] = att.astype(BF16).reshape(slots, GROUP, HEAD_DIM)


def backward_kernel(
    lo_ref, mid_ref, g_ref, cos_ref, sin_ref, pq_ref, lq_ref, kp_ref, ot_ref, lse_ref,
    q_ref, k_ref, v_ref, qt_ref, kt_ref, out_ref, dk_ref, dv_ref,
):
    t = pl.program_id(0)
    slots = g_ref.shape[0]
    tile = slots * GROUP
    chunk = q_ref.shape[1]
    per = tile // chunk
    scaling = HEAD_DIM**-0.5
    grads = g_ref[...].reshape(tile, HEAD_DIM)
    for c in range(per):
        dk_ref[t * per + c] = jnp.zeros((chunk, HEAD_DIM), F32)
        dv_ref[t * per + c] = jnp.zeros((chunk, HEAD_DIM), F32)
    parts = []
    for c in range(per):
        index = t * per + c
        do = grads[c * chunk : (c + 1) * chunk]
        dot32 = do.astype(F32).T
        dot16 = dot32.astype(BF16)
        delta = jnp.sum(dot32 * ot_ref[c], axis=0, keepdims=True)
        lse = lse_ref[c]
        q, qt = q_ref[index], qt_ref[index]
        query_pos, query_lo = pq_ref[c], lq_ref[c]

        def step(kc, dqt, masked):
            probs = jnp.exp(dot_nn(k_ref[kc], qt) - lse)
            if masked:
                key_pos = kp_ref[kc]
                visible = (key_pos <= query_pos) & (key_pos >= query_lo)
                probs = jnp.where(visible, probs, 0.0)
            dv_ref[kc] += dot_nn(probs.astype(BF16), do)
            prob_grad = dot_nn(v_ref[kc], dot16)
            score_grad = (probs * (prob_grad - delta)).astype(BF16)
            dk_ref[kc] += dot_nn(score_grad, q)
            return dqt + dot_nn(kt_ref[kc], score_grad)

        dqt = jnp.zeros((HEAD_DIM, chunk), F32)
        dqt = lax.fori_loop(lo_ref[t], mid_ref[t], lambda i, s: step(i, s, True), dqt)
        dqt = lax.fori_loop(mid_ref[t], t * per, lambda i, s: step(i, s, False), dqt)
        dqt = lax.fori_loop(t * per, (t + 1) * per, lambda i, s: step(i, s, True), dqt)
        parts.append(rope_t(dqt * scaling, cos_ref[index], -sin_ref[index]).T)
    dq = parts[0] if per == 1 else jnp.concatenate(parts, axis=0)
    here = pl.ds(pl.multiple_of(t * GROUP, GROUP), GROUP)
    out_ref[:, here, :HEAD_DIM] = dq.astype(BF16).reshape(slots, GROUP, HEAD_DIM)

    @pl.when(t == pl.num_programs(0) - 1)
    def _():
        def finish(u, carry):
            rows = []
            for c in range(per):
                index = u * per + c
                dkt = rope_t(dk_ref[index].T * scaling, cos_ref[index], -sin_ref[index])
                rows.append(jnp.concatenate([dkt.T, dv_ref[index]], axis=1))
            both = rows[0] if per == 1 else jnp.concatenate(rows, axis=0)
            place = pl.ds(pl.multiple_of(u * GROUP, GROUP), GROUP)
            out_ref[:, place, HEAD_DIM:] = both.astype(BF16).reshape(slots, GROUP, 2 * HEAD_DIM)
            return carry

        lax.fori_loop(0, pl.num_programs(0), finish, 0)


def whole_block(shape):
    zeros = (0,) * len(shape)
    return pl.BlockSpec(tuple(shape), lambda t, *refs: zeros)


def tile_block(shape, axis):
    def place(t, *refs):
        return tuple(t if i == axis else 0 for i in range(len(shape)))

    return pl.BlockSpec(tuple(shape), place)


def attention_meta(positions, seq_lengths, chunk):
    tiles, tile = positions.shape
    count = tiles * tile // chunk
    per = tile // chunk
    opening, place = seq_meta(positions, seq_lengths)
    frequency = 10000.0 ** (-2.0 * jnp.arange(ROT // 2, dtype=F32) / ROT)
    angles = place.astype(F32).reshape(count, 1, chunk) * frequency[None, :, None]
    ends = jnp.arange(tiles, dtype=jnp.int32) * tile
    first_open, _ = seq_meta(ends, seq_lengths)
    last_open, _ = seq_meta(ends + tile - 1, seq_lengths)
    own = jnp.arange(tiles, dtype=jnp.int32) * per
    low = (first_open // tile) * per
    middle = jnp.minimum(((last_open + tile - 1) // tile) * per, own)
    return dict(
        low=low.astype(jnp.int32),
        middle=middle.astype(jnp.int32),
        cosine=jnp.cos(angles),
        sine=jnp.sin(angles),
        query_pos=positions.reshape(count, 1, chunk),
        query_lo=opening.reshape(count, 1, chunk),
        key_pos=positions.reshape(count, chunk, 1),
    )


def attention_forward(zq, bias, meta):
    slots, rows, width = zq.shape
    tile = slots * GROUP
    tiles = rows // GROUP
    count, _, chunk = meta["query_pos"].shape
    per = tile // chunk
    half = ROT // 2
    nat = jax.ShapeDtypeStruct((count, chunk, HEAD_DIM), BF16)
    turned = jax.ShapeDtypeStruct((count, HEAD_DIM, chunk), BF16)
    shapes = [
        jax.ShapeDtypeStruct((slots, rows, HEAD_DIM), BF16),
        jax.ShapeDtypeStruct((count, HEAD_DIM, chunk), F32),
        jax.ShapeDtypeStruct((count, 1, chunk), F32),
        nat, nat, nat, turned, turned,
    ]
    return pl.pallas_call(
        forward_kernel,
        out_shape=shapes,
        grid_spec=pltpu.PrefetchScalarGridSpec(
            num_scalar_prefetch=2,
            grid=(tiles,),
            in_specs=[
                tile_block((slots, GROUP, width), 1),
                whole_block((1, width)),
                tile_block((per, half, chunk), 0),
                tile_block((per, half, chunk), 0),
                tile_block((per, 1, chunk), 0),
                tile_block((per, 1, chunk), 0),
                whole_block((count, chunk, 1)),
            ],
            out_specs=[
                tile_block((slots, GROUP, HEAD_DIM), 1),
                tile_block((per, HEAD_DIM, chunk), 0),
                tile_block((per, 1, chunk), 0),
                whole_block(nat.shape),
                whole_block(nat.shape),
                whole_block(nat.shape),
                whole_block(turned.shape),
                whole_block(turned.shape),
            ],
            scratch_shapes=[pltpu.VMEM(turned.shape, BF16)],
        ),
        compiler_params=pltpu.CompilerParams(
            dimension_semantics=("arbitrary",), vmem_limit_bytes=58 * 1024 * 1024
        ),
        cost_estimate=pl.CostEstimate(
            flops=30_000_000_000, bytes_accessed=12_000_000, transcendentals=6_000_000
        ),
        name="attention_forward",
    )(
        meta["low"], meta["middle"], zq, bias, meta["cosine"], meta["sine"],
        meta["query_pos"], meta["query_lo"], meta["key_pos"],
    )


def attention_backward(heads_grad, meta, saved):
    slots, rows, _ = heads_grad.shape
    tile = slots * GROUP
    tiles = rows // GROUP
    count, _, chunk = meta["query_pos"].shape
    per = tile // chunk
    half = ROT // 2
    ot, lse, q, k, v, qt, kt = saved
    return pl.pallas_call(
        backward_kernel,
        out_shape=jax.ShapeDtypeStruct((slots, rows, 3 * HEAD_DIM), BF16),
        grid_spec=pltpu.PrefetchScalarGridSpec(
            num_scalar_prefetch=2,
            grid=(tiles,),
            in_specs=[
                tile_block((slots, GROUP, HEAD_DIM), 1),
                whole_block((count, half, chunk)),
                whole_block((count, half, chunk)),
                tile_block((per, 1, chunk), 0),
                tile_block((per, 1, chunk), 0),
                whole_block((count, chunk, 1)),
                tile_block((per, HEAD_DIM, chunk), 0),
                tile_block((per, 1, chunk), 0),
                whole_block(q.shape),
                whole_block(k.shape),
                whole_block(v.shape),
                whole_block(qt.shape),
                whole_block(kt.shape),
            ],
            out_specs=whole_block((slots, rows, 3 * HEAD_DIM)),
            scratch_shapes=[
                pltpu.VMEM((count, chunk, HEAD_DIM), F32),
                pltpu.VMEM((count, chunk, HEAD_DIM), F32),
            ],
        ),
        compiler_params=pltpu.CompilerParams(
            dimension_semantics=("arbitrary",), vmem_limit_bytes=62 * 1024 * 1024
        ),
        cost_estimate=pl.CostEstimate(
            flops=60_000_000_000, bytes_accessed=12_000_000, transcendentals=6_000_000
        ),
        name="attention_backward",
    )(
        meta["low"], meta["middle"], heads_grad, meta["cosine"], meta["sine"],
        meta["query_pos"], meta["query_lo"], meta["key_pos"], ot, lse, q, k, v, qt, kt,
    )


def gather_rows(rows, core, pieces, count):
    found = []
    for (begin, end), order in pieces:
        held = rows[begin:end][None]
        for mask in order[:-1]:
            held = jnp.concatenate([held, swap(held, mask, count)], axis=0)
        last = swap(held, order[-1], count)
        found.append([held, last, swap(held, core, count), swap(last, core, count)])
    return found


def reduce_rows(sent, kept, order, count):
    for mask in order[::-1][:-1]:
        total = kept.astype(F32) + swap(sent, mask, count).astype(F32)
        middle = total.shape[0] // 2
        sent, kept = total[middle:].astype(BF16), total[:middle].astype(BF16)
    total = kept.astype(F32) + swap(sent, order[0], count).astype(F32)
    return total[0]


def gather_small(block, stages, count):
    for masks, axis_len in stages:
        parts = [block if m == 0 else swap(block, m, count) for m in masks]
        block = jnp.stack(parts, axis=0)
    return block.reshape((-1,) + block.shape[len(stages) :])


def reduce_small(block, stages, count):
    for masks, axis_len in stages[::-1]:
        block = block.reshape((len(masks), -1) + block.shape[1:])
        total = block[0]
        for i, m in enumerate(masks):
            if m:
                total = total + swap(block[i], m, count)
        block = total
    return block[0]


def gelu_tanh(values):
    return jax.nn.gelu(values, approximate=True)


def gelu_back(hidden, act_grad):
    _, pullback = jax.vjp(gelu_tanh, hidden)
    return pullback(act_grad)[0]


def pairwise(block, core, count):
    half = block.shape[0] // 2
    return block[:half], swap(block[half:], core, count)


def per_device(
    layer_in, out_grad, norm_gain, norm_bias, w_qkv, b_qkv, w_out, b_out, w_up, b_up,
    w_down, b_down, seq_lengths, token_place,
):
    heads, blks = lax.axis_size("head"), lax.axis_size("blk")
    count = heads * blks
    me = lax.axis_index("head") * blks + lax.axis_index("blk")
    rows, width = layer_in.shape
    features = w_qkv.shape[1]
    hidden_units = w_up.shape[0]
    owners = HEAD_DIM // features
    core, pieces = plan_of(heads, blks)
    stages = [
        ([m for m in range(blks)], blks),
        ([m * blks for m in range(heads)], heads),
    ]

    place = token_place.reshape(count, rows)
    own_place = lax.dynamic_slice_in_dim(place, me, 1, 0)[0]
    order_hot = (
        own_place[None, :] // count == jnp.arange(rows, dtype=jnp.int32)[:, None]
    ).astype(BF16)
    x_sorted = dot_nn(order_hot, layer_in)
    g_sorted = dot_nn(order_hot, out_grad).astype(BF16)

    vectors = jnp.stack([norm_gain, norm_bias, b_out, b_down])
    vectors = gather_small(vectors, stages, count)
    absolute = me ^ jnp.arange(count, dtype=jnp.int32)
    choose = (absolute[None, :] == jnp.arange(count, dtype=jnp.int32)[:, None]).astype(BF16)
    vectors = dot_nn(choose, vectors.reshape(count, -1)).reshape(count, 4, -1)
    vectors = jnp.transpose(vectors, (1, 0, 2)).reshape(4, width)
    gain, offset, out_bias, down_bias = (vectors[i][None] for i in range(4))

    center = jnp.mean(x_sorted, axis=-1, keepdims=True)
    centered = x_sorted - center
    variance = jnp.mean(centered * centered, axis=-1, keepdims=True)
    inverse = lax.rsqrt(variance + 1e-05)
    x_hat = centered * inverse
    normed = (x_hat * gain + offset).astype(BF16)

    normed_all = gather_rows(normed, core, pieces, count)
    g_all = gather_rows(g_sorted, core, pieces, count)

    inside = place // count
    sorted_place = jnp.sum(
        jnp.where(
            inside[:, None, :] == jnp.arange(rows, dtype=jnp.int32)[None, :, None],
            place[:, None, :],
            0,
        ),
        axis=2,
    )
    chunks = []
    for (begin, end), order in pieces:
        slots = me ^ jnp.array(slot_masks(core, order), dtype=jnp.int32)
        chunks.append(sorted_place[slots, begin:end])
    positions = jnp.concatenate(chunks, axis=1)
    tiles = rows // GROUP
    positions = jnp.transpose(positions.reshape(count, tiles, GROUP), (1, 0, 2))
    positions = positions.reshape(tiles, count * GROUP)
    meta = attention_meta(positions, seq_lengths, min(CHUNK, count * GROUP))

    w_in = jnp.concatenate([w_qkv.reshape(3 * features, width), w_up], axis=0)
    w_back = jnp.concatenate([w_out, w_down], axis=0)
    w_in_other = swap(w_in, core, count)
    w_back_other = swap(w_back, core, count)

    def all_rows(buffers, weight):
        found = []
        for (begin, end), parts in zip([p[0] for p in pieces], buffers):
            blocks = [
                dot_nt(b.reshape(-1, width), weight).reshape(-1, end - begin, weight.shape[0])
                for b in parts
            ]
            found.append(jnp.concatenate(blocks, axis=0))
        return jnp.concatenate(found, axis=1)

    z = all_rows(normed_all, w_in)
    zq, hidden = z[:, :, : 3 * features], z[:, :, 3 * features :]
    hidden = hidden + b_up.astype(F32)
    active = gelu_tanh(hidden).astype(BF16)
    bias = b_qkv.astype(F32)

    member = me % owners
    member_order = member ^ jnp.arange(owners, dtype=jnp.int32)

    def from_owners(block):
        found = [block]
        for extra in range(1, owners):
            other = swap(block, extra, count)
            flipped = []
            at = 0
            for (begin, end), order in pieces:
                masks = slot_masks(core, order)
                where = [masks.index(m ^ extra) for m in masks]
                flipped.append(other[jnp.array(where), begin:end])
            found.append(jnp.concatenate(flipped, axis=1))
        stacked = jnp.stack(found)[member_order]
        return jnp.moveaxis(stacked, 0, -2).reshape(block.shape[:-1] + (HEAD_DIM,))

    def own_features(block):
        if owners == 1:
            return block
        shape = block.shape
        split = block.reshape(shape[:2] + (-1, owners, features))
        return lax.dynamic_index_in_dim(split, member, 3, False).reshape(shape[:2] + (-1,))

    if owners > 1:
        zq = zq.reshape(zq.shape[:2] + (3, features)) + bias
        zq = from_owners(zq.astype(F32)).reshape(zq.shape[:2] + (3 * HEAD_DIM,))
        bias = jnp.zeros((3, HEAD_DIM), F32)
    attended, *saved = attention_forward(zq, bias.reshape(1, 3 * HEAD_DIM), meta)
    attended = own_features(attended)

    def partial_sums(first, second, own_weight, other_weight, cut):
        first_own, first_other = pairwise(first, core, count)
        second_own, second_other = pairwise(second, core, count)
        both = jnp.concatenate([first_own, first_other, second_own, second_other], axis=2)
        weight = jnp.concatenate(
            [own_weight[:cut], other_weight[:cut], own_weight[cut:], other_weight[cut:]], axis=0
        )
        middle = both.shape[0] // 2
        found = []
        for (begin, end), order in pieces:
            def product(part):
                flat = part[:, begin:end].reshape(-1, weight.shape[0])
                return dot_nn(flat, weight).astype(BF16).reshape(-1, end - begin, width)

            found.append(reduce_rows(product(both[middle:]), product(both[:middle]), order, count))
        return jnp.concatenate(found, axis=0)

    mixed = partial_sums(attended, active, w_back, w_back_other, features)

    back = all_rows(g_all, w_back)
    heads_grad = back[:, :, :features].astype(BF16)
    hidden_grad = gelu_back(hidden, back[:, :, features:]).astype(BF16)
    if owners > 1:
        heads_grad = from_owners(heads_grad[:, :, None, :]).reshape(heads_grad.shape[:2] + (HEAD_DIM,))
    qkv_grad = attention_backward(heads_grad, meta, saved[:7])
    qkv_grad = own_features(qkv_grad)
    normed_grad = partial_sums(qkv_grad, hidden_grad, w_in, w_in_other, 3 * features)

    def weight_sums(rows_left, buffers):
        total = 0.0
        for (begin, end), parts in zip([p[0] for p in pieces], buffers):
            left = rows_left[:, begin:end].reshape(-1, rows_left.shape[2])
            right = jnp.concatenate(parts, axis=0).reshape(-1, width)
            total = total + dot_tn(left, right)
        return total

    back_grad = weight_sums(jnp.concatenate([attended, active], axis=2), g_all)
    in_grad = weight_sums(jnp.concatenate([qkv_grad, hidden_grad], axis=2), normed_all)
    b_in = jnp.concatenate(
        [
            jnp.sum(qkv_grad.astype(F32), axis=(0, 1)),
            jnp.sum(hidden_grad.astype(F32), axis=(0, 1)),
        ]
    )

    layer_out = (x_sorted + mixed + out_bias + down_bias).astype(BF16)
    layer_out = dot_tn(order_hot, layer_out).astype(BF16)
    e = normed_grad * gain
    input_part = inverse * (
        e
        - jnp.mean(e, axis=-1, keepdims=True)
        - x_hat * jnp.mean(e * x_hat, axis=-1, keepdims=True)
    )
    input_grad = (g_sorted.astype(F32) + input_part).astype(BF16)
    input_grad = dot_tn(order_hot, input_grad).astype(BF16)
    sums = jnp.stack(
        [
            jnp.sum(normed_grad * x_hat, axis=0),
            jnp.sum(normed_grad, axis=0),
            jnp.sum(g_sorted.astype(F32), axis=0),
        ]
    )
    sums = jnp.transpose(sums.reshape(3, count, -1), (1, 0, 2))[absolute]
    sums = reduce_small(sums, stages, count)
    return (
        layer_out,
        input_grad,
        sums[0],
        sums[1],
        in_grad[: 3 * features].reshape(3, features, width),
        b_in[: 3 * features].reshape(3, features),
        back_grad[:features],
        sums[2],
        in_grad[3 * features :],
        b_in[3 * features :],
        back_grad[features:],
        sums[2],
    )


def solution(mesh):
    rows, vector = P(AXES, None), P(AXES)
    qkv, qkv_bias = P(None, AXES, None), P(None, AXES)
    in_specs = (
        rows, rows, vector, vector, qkv, qkv_bias, rows, vector, rows, vector, rows, vector,
        P(), P(),
    )
    out_specs = (
        rows, rows, vector, vector, qkv, qkv_bias, rows, vector, rows, vector, rows, vector,
    )
    return jax.shard_map(
        per_device, mesh=mesh, in_specs=in_specs, out_specs=out_specs, check_vma=False
    )
```

time: 5590 us -> 807 us (0.14)
  waiting for transfers between devices: 4750 us -> 234 us
  blocking collectives: 257 us -> 0 us
  matrix products: 349 us -> 103 us
  local copies, waits for them, and re-layouts: 78.1 us -> 269 us
  starting transfers between devices: 20.2 us -> 103 us
  other arithmetic: 106 us -> 40.3 us
    reduce_scatter x4 -> x0, waiting for transfers between devices: 4070 us -> none  [the longest x1 1410 us: per_device(): lax.psum_scatter(w_up_g, ('head', 'blk'), scatter_dimension=0, tiled=True)]
    dot_general x68 -> x47, matrix products: 349 us -> 103 us  [the longest x24 52.6 us: dot_nt(): lax.dot_general(a, b, (((1,), (1,)), ((), ())), preferred_element_type=F32)]
    ppermute x16 -> x86, waiting for transfers between devices: 478 us -> 234 us  [swap(): return lax.ppermute(block, AXES, [(i, i ^ mask) for i in range(count)])]
    gather x0 -> x385, local copies, waits for them, and re-layouts: none -> 192 us
    all_gather x5 -> x0, waiting for transfers between devices: 161 us -> none  [the longest x1 104 us: attention_forward(): kv_piece = lax.all_gather(qkv_heads[:, 1:], 'blk', axis=0, tiled=True)]
    all_gather x2 -> x0, blocking collectives: 134 us -> none  [the longest x1 70.7 us: per_device(): lax.all_gather(b_qkv, ('head', 'blk'), axis=1, tiled=True)]
    ppermute x16 -> x86, starting transfers between devices: 7.7 us -> 103 us  [swap(): return lax.ppermute(block, AXES, [(i, i ^ mask) for i in range(count)])]
    unnamed x2 -> x0, blocking collectives: 87.7 us -> none
  transfers between devices with their start and end apart: 29 -> 86, of which waited for: 26 -> 27; matrix products, arithmetic and copies ran while one was open for 9% -> 49% of each run, Pallas kernels for 0% -> 6%
where the time goes in v1:
time: 807 us; the launch traced here: 801 us
  local copies, waits for them, and re-layouts  269 us (33%)
  waiting for transfers between devices  234 us (29%)
  starting transfers between devices  103 us (13%)
  matrix products  103 us (13%)
  Pallas kernels  47.6 us (6%)
  other arithmetic  40.3 us (5%)
    ppermute x86, waiting for transfers between devices, swap(): return lax.ppermute(block, AXES, [(i, i ^ mask) for i in range(count)])  234 us
    gather x384, local copies, waits for them, and re-layouts  191 us
    ppermute x86, starting transfers between devices, swap(): return lax.ppermute(block, AXES, [(i, i ^ mask) for i in range(count)])  103 us
    dot_general x24, matrix products, dot_nt(): lax.dot_general(a, b, (((1,), (1,)), ((), ())), preferred_element_type=F32)  52.6 us
    unnamed x178, local copies, waits for them, and re-layouts  30.9 us
    dot_general x8, matrix products, dot_tn(): lax.dot_general(a, b, (((0,), (0,)), ((), ())), preferred_element_type=F32)  28.8 us
    pallas_call x1, Pallas kernels, attention_backward(): pl.pallas_call(backward_kernel, out_shape=jax.ShapeDtypeStruct((slots, ro...  25.1 us
    pallas_call x1, Pallas kernels, attention_forward(): pl.pallas_call(forward_kernel, out_shape=shapes, grid_spec=pltpu.Prefetch...  22.5 us
  transfers between devices with their start and end apart: 86, of which 27 were waited for; matrix products, arithmetic and copies ran while one was open for 49% of the time, Pallas kernels for 6%

profile of v1, /device:TPU:0, one launch (start us, length us, event | category | flops | bytes accessed | tf_op | source)
XLA Modules:
  0.0 800.7 jit_solution(5281303127892930674)
XLA Ops:
  16.1 63.8 %while.4 = (s32[]{:T(128)}, s32[32,128]{1,0:T(8,128)S(1)}, s32[32,2]{0,1:T(2,128)S(1)}, s32[32,48]{1,0:T(8,128)S(1)}, s32[]{:T(128)}, /*index=5*/s32[]{:T(128)}) while((s32[]{:T(128)}, s32[32,128]{1,0:T(8,128)S(1)}, s32[32,2]{0,1:T(2,128)S(1)}, s32[32,48]{1,0:T(8,128)S(1)}, s32[]{:T(128)}, /*index=5*/s32[]{:T(128)}) %tuple.97), condition=%wide.while_cond.1, body=%wide.while_body.1.sunk | while | flops 2 | bytes 889 | solution.py:441
  79.9 63.8 %while.3 = (s32[]{:T(128)}, s32[32,128]{1,0:T(8,128)S(1)}, s32[32,2]{0,1:T(2,128)S(1)}, s32[32,48]{1,0:T(8,128)S(1)}, s32[]{:T(128)}, /*index=5*/s32[]{:T(128)}) while((s32[]{:T(128)}, s32[32,128]{1,0:T(8,128)S(1)}, s32[32,2]{0,1:T(2,128)S(1)}, s32[32,48]{1,0:T(8,128)S(1)}, s32[]{:T(128)}, /*index=5*/s32[]{:T(128)}) %tuple.105), condition=%wide.while_cond, body=%wide.while_body.sunk | while | flops 2 | bytes 889 | solution.py:441
  143.7 63.8 %while.5 = (s32[]{:T(128)}, s32[32,128]{1,0:T(8,128)S(1)}, s32[32,2]{0,1:T(2,128)S(1)}, s32[32,32]{1,0:T(8,128)S(1)}, s32[]{:T(128)}, /*index=5*/s32[]{:T(128)}) while((s32[]{:T(128)}, s32[32,128]{1,0:T(8,128)S(1)}, s32[32,2]{0,1:T(2,128)S(1)}, s32[32,32]{1,0:T(8,128)S(1)}, s32[]{:T(128)}, /*index=5*/s32[]{:T(128)}) %tuple.106), condition=%wide.while_cond.2, body=%wide.while_body.2.sunk | while | flops 2 | bytes 633 | solution.py:441
  244.1 9.5 %collective-permute-done.22 = bf16[1,32,2048]{2,1,0:T(8,128)(2,1)S(1)} collective-permute-done((bf16[1,32,2048]{2,1,0:T(8,128)(2,1)S(1)}, bf16[1,32,2048]{2,1,0:T(8,128)(2,1)S(1)}, u32[]{:S(2)}, u32[]{:S(2)}) %collective-permute-start.22) | collective-permute-done | bytes 131104 | tf_op jit(solution)/shard_map/ppermute | solution.py:19
  259.3 14.0 %collective-permute-done.16 = bf16[1,48,2048]{2,1,0:T(8,128)(2,1)S(1)} collective-permute-done((bf16[1,48,2048]{2,1,0:T(8,128)(2,1)S(1)}, bf16[1,48,2048]{2,1,0:T(8,128)(2,1)S(1)}, u32[]{:S(2)}, u32[]{:S(2)}) %collective-permute-start.16) | collective-permute-done | bytes 196640 | tf_op jit(solution)/shard_map/ppermute | solution.py:19
  299.9 8.7 %collective-permute-done.57 = bf16[4,32,2048]{2,1,0:T(8,128)(2,1)S(1)} collective-permute-done((bf16[4,32,2048]{2,1,0:T(8,128)(2,1)S(1)}, bf16[4,32,2048]{2,1,0:T(8,128)(2,1)S(1)}, u32[]{:S(2)}, u32[]{:S(2)}) %collective-permute-start.57) | collective-permute-done | bytes 524320 | tf_op jit(solution)/shard_map/ppermute | solution.py:19
  333.1 7.9 collective-permute-done.18
  354.3 9.2 %collective-permute-done.58 = bf16[8,32,2048]{2,1,0:T(8,128)(2,1)S(1)} collective-permute-done((bf16[8,32,2048]{2,1,0:T(8,128)(2,1)S(1)}, bf16[8,32,2048]{2,1,0:T(8,128)(2,1)S(1)}, u32[]{:S(2)}, u32[]{:S(2)}) %collective-permute-start.58) | collective-permute-done | bytes 1048608 | tf_op jit(solution)/shard_map/ppermute | solution.py:19
  372.5 11.3 %collective-permute-done.25 = bf16[8,32,2048]{2,1,0:T(8,128)(2,1)S(1)} collective-permute-done((bf16[8,32,2048]{2,1,0:T(8,128)(2,1)S(1)}, bf16[8,32,2048]{2,1,0:T(8,128)(2,1)S(1)}, u32[]{:S(2)}, u32[]{:S(2)}) %collective-permute-start.25) | collective-permute-done | bytes 1048608 | tf_op jit(solution)/shard_map/ppermute | solution.py:19
  392.1 12.3 %collective-permute-done.46 = bf16[8,48,2048]{2,1,0:T(8,128)(2,1)S(1)} collective-permute-done((bf16[8,48,2048]{2,1,0:T(8,128)(2,1)S(1)}, bf16[8,48,2048]{2,1,0:T(8,128)(2,1)S(1)}, u32[]{:S(2)}, u32[]{:S(2)}) %collective-permute-start.46) | collective-permute-done | bytes 1572896 | tf_op jit(solution)/shard_map/ppermute | solution.py:19
  419.7 18.2 %collective-permute-done.13 = bf16[8,48,2048]{2,1,0:T(8,128)(2,1)S(1)} collective-permute-done((bf16[8,48,2048]{2,1,0:T(8,128)(2,1)S(1)}, bf16[8,48,2048]{2,1,0:T(8,128)(2,1)S(1)}, u32[]{:S(2)}, u32[]{:S(2)}) %collective-permute-start.13) | collective-permute-done | bytes 1572896 | tf_op jit(solution)/shard_map/ppermute | solution.py:19
  477.0 5.4 convert_reduce_fusion
  485.9 22.5 %attention_forward.1 = (bf16[32,128,64]{2,1,0:T(8,128)(2,1)}, f32[8,64,512]{2,1,0:T(8,128)}, f32[8,1,512]{2,1,0:T(1,128)}, bf16[8,512,64]{2,1,0:T(8,128)(2,1)}, ...) custom-call(s32[8]{0:T(128)} %get-tuple-element.151.lo_ref, ...), custom_call_target="tpu_custom_call" | custom-call | flops 30000001024 | bytes 12000000 | tf_op jit(solution)/shard_map/attention_forward/pallas_call | solution.py:246
  510.5 25.1 %attention_backward.1 = bf16[32,128,192]{2,1,0:T(8,128)(2,1)} custom-call(s32[8]{0:T(128)} %get-tuple-element.151.lo_ref, s32[8]{0:T(128)} %get-tuple-element.152.mid_ref, bf16[32,128,64]{2,1,0:T(8,128)(2,1)} %slice.706.g_ref, f32[8,16,512]{2,1,0:T(8,128)} %get-tuple-element.134.cos_ref, f32[8,16,512]{2,1,0:T(8,128)} %get-tuple-element.133.sin_ref, ...), custom_call_target="tpu_custom_call" | custom-call | flops 60000002048 | bytes 12000000 | tf_op jit(solution)/shard_map/attention_backward/pallas_call | solution.py:294
  545.5 5.3 convolution_bitcast_fusion.1
  552.9 5.5 fusion.43
  559.8 5.9 fusion.40
  616.2 17.9 %collective-permute-done.72 = bf16[8,32,2048]{2,1,0:T(8,128)(2,1)S(1)} collective-permute-done((bf16[8,32,2048]{2,1,0:T(8,128)(2,1)S(1)}, bf16[8,32,2048]{2,1,0:T(8,128)(2,1)S(1)}, u32[]{:S(2)}, u32[]{:S(2)}) %collective-permute-start.72) | collective-permute-done | bytes 1048608 | tf_op jit(solution)/shard_map/ppermute | solution.py:19
  636.2 35.1 %collective-permute-done.40 = bf16[4,32,2048]{2,1,0:T(8,128)(2,1)S(1)} collective-permute-done((bf16[4,32,2048]{2,1,0:T(8,128)(2,1)S(1)}, bf16[4,32,2048]{2,1,0:T(8,128)(2,1)S(1)}, u32[]{:S(2)}, u32[]{:S(2)}) %collective-permute-start.40) | collective-permute-done | bytes 524320 | tf_op jit(solution)/shard_map/ppermute | solution.py:19
  676.8 7.6 collective-permute-done.73
  690.6 14.5 %collective-permute-done.74 = bf16[2,32,2048]{2,1,0:T(8,128)(2,1)S(1)} collective-permute-done((bf16[2,32,2048]{2,1,0:T(8,128)(2,1)S(1)}, bf16[2,32,2048]{2,1,0:T(8,128)(2,1)S(1)}, u32[]{:S(2)}, u32[]{:S(2)}) %collective-permute-start.74) | collective-permute-done | bytes 262176 | tf_op jit(solution)/shard_map/ppermute | solution.py:19
  707.6 12.8 %collective-permute-done.42 = bf16[1,32,2048]{2,1,0:T(8,128)(2,1)S(1)} collective-permute-done((bf16[1,32,2048]{2,1,0:T(8,128)(2,1)S(1)}, bf16[1,32,2048]{2,1,0:T(8,128)(2,1)S(1)}, u32[]{:S(2)}, u32[]{:S(2)}) %collective-permute-start.42) | collective-permute-done | bytes 131104 | tf_op jit(solution)/shard_map/ppermute | solution.py:19
  735.2 8.0 %collective-permute-done.33 = bf16[2,48,2048]{2,1,0:T(8,128)(2,1)S(1)} collective-permute-done((bf16[2,48,2048]{2,1,0:T(8,128)(2,1)S(1)}, bf16[2,48,2048]{2,1,0:T(8,128)(2,1)S(1)}, u32[]{:S(2)}, u32[]{:S(2)}) %collective-permute-start.33) | collective-permute-done | bytes 393248 | tf_op jit(solution)/shard_map/ppermute | solution.py:19
  755.6 15.4 %collective-permute-done.67 = bf16[1,48,2048]{2,1,0:T(8,128)(2,1)S(1)} collective-permute-done((bf16[1,48,2048]{2,1,0:T(8,128)(2,1)S(1)}, bf16[1,48,2048]{2,1,0:T(8,128)(2,1)S(1)}, u32[]{:S(2)}, u32[]{:S(2)}) %collective-permute-start.67) | collective-permute-done | bytes 196640 | tf_op jit(solution)/shard_map/ppermute | solution.py:19
  (921 shorter events, 525.4 us)
Async XLA Ops:
  1.5 225.5 %collective-permute-start.5 = (bf16[4,64]{1,0:T(4,128)(2,1)S(1)}, bf16[4,64]{1,0:T(4,128)(2,1)S(1)}, u32[]{:S(2)}, u32[]{:S(2)}) collective-permute-start(bf16[4,64]{1,0:T(4,128)(2,1)S(1)} %get-tuple-element.84), channel_id=1, source_target_pairs={{0,6},{1,7},{2,4},{3,5},{4,2},{5,3},{6,0},{7,1},{8,14},{9,15},{10,... | collective-permute-start | bytes 1544 | tf_op jit(solution)/shard_map/ppermute | solution.py:19
  6.6 220.4 %collective-permute-start.4 = (bf16[4,64]{1,0:T(4,128)(2,1)S(1)}, bf16[4,64]{1,0:T(4,128)(2,1)S(1)}, u32[]{:S(2)}, u32[]{:S(2)}) collective-permute-start(bf16[4,64]{1,0:T(4,128)(2,1)S(1)} %get-tuple-element.84), channel_id=1, source_target_pairs={{0,5},{1,4},{2,7},{3,6},{4,1},{5,0},{6,3},{7,2},{8,13},{9,12},{10,... | collective-permute-start | bytes 1544 | tf_op jit(solution)/shard_map/ppermute | solution.py:19
  7.0 219.0 %collective-permute-start.3 = (bf16[4,64]{1,0:T(4,128)(2,1)S(1)}, bf16[4,64]{1,0:T(4,128)(2,1)S(1)}, u32[]{:S(2)}, u32[]{:S(2)}) collective-permute-start(bf16[4,64]{1,0:T(4,128)(2,1)S(1)} %get-tuple-element.84), channel_id=1, source_target_pairs={{0,4},{1,5},{2,6},{3,7},{4,0},{5,1},{6,2},{7,3},{8,12},{9,13},{10,... | collective-permute-start | bytes 1544 | tf_op jit(solution)/shard_map/ppermute | solution.py:19
  10.5 213.5 %collective-permute-start.2 = (bf16[4,64]{1,0:T(4,128)(2,1)S(1)}, bf16[4,64]{1,0:T(4,128)(2,1)S(1)}, u32[]{:S(2)}, u32[]{:S(2)}) collective-permute-start(bf16[4,64]{1,0:T(4,128)(2,1)S(1)} %get-tuple-element.84), channel_id=1, source_target_pairs={{0,3},{1,2},{2,1},{3,0},{4,7},{5,6},{6,5},{7,4},{8,11},{9,10},{10,... | collective-permute-start | bytes 1544 | tf_op jit(solution)/shard_map/ppermute | solution.py:19
  10.5 208.0 %collective-permute-start = (bf16[4,64]{1,0:T(4,128)(2,1)S(1)}, bf16[4,64]{1,0:T(4,128)(2,1)S(1)}, u32[]{:S(2)}, u32[]{:S(2)}) collective-permute-start(bf16[4,64]{1,0:T(4,128)(2,1)S(1)} %get-tuple-element.84), channel_id=1, source_target_pairs={{0,1},{1,0},{2,3},{3,2},{4,5},{5,4},{6,7},{7,6},{8,9},{9,8},{10,11... | collective-permute-start | bytes 1544 | tf_op jit(solution)/shard_map/ppermute | solution.py:19
  238.0 82.1 %collective-permute-start.30 = (bf16[320,2048]{1,0:T(8,128)(2,1)}, bf16[320,2048]{1,0:T(8,128)(2,1)}, u32[]{:S(2)}, u32[]{:S(2)}) collective-permute-start(bf16[320,2048]{1,0:T(8,128)(2,1)} %constant_dynamic-update-slice_fusion.8), channel_id=1, source_target_pairs={{0,8},{1,9},{2,10},{3,11},{4,12},{5,13},{6,14},{7,15},{8,0},{9,1},... | collective-permute-start | bytes 3932168 | tf_op jit(solution)/shard_map/ppermute | solution.py:19
  238.1 108.5 %collective-permute-start.63 = (bf16[448,2048]{1,0:T(8,128)(2,1)}, bf16[448,2048]{1,0:T(8,128)(2,1)}, u32[]{:S(2)}, u32[]{:S(2)}) collective-permute-start(bf16[448,2048]{1,0:T(8,128)(2,1)} %pad_maximum_fusion.4), channel_id=1, source_target_pairs={{0,8},{1,9},{2,10},{3,11},{4,12},{5,13},{6,14},{7,15},{8,0},{9,1},... | collective-permute-start | bytes 5505032 | tf_op jit(solution)/shard_map/ppermute | solution.py:19
  341.0 42.7 %collective-permute-start.25 = (bf16[8,32,2048]{2,1,0:T(8,128)(2,1)S(1)}, bf16[8,32,2048]{2,1,0:T(8,128)(2,1)S(1)}, u32[]{:S(2)}, u32[]{:S(2)}) collective-permute-start(bf16[8,32,2048]{2,1,0:T(8,128)(2,1)S(1)} %pad_maximum_fusion.11), channel_id=1, source_target_pairs={{0,2},{1,3},{2,0},{3,1},{4,6},{5,7},{6,4},{7,5},{8,10},{9,11},{10,... | collective-permute-start | bytes 3145736 | tf_op jit(solution)/shard_map/ppermute | solution.py:19
  342.4 41.5 %collective-permute-start.26 = (bf16[8,32,2048]{2,1,0:T(8,128)(2,1)S(1)}, bf16[8,32,2048]{2,1,0:T(8,128)(2,1)S(1)}, u32[]{:S(2)}, u32[]{:S(2)}) collective-permute-start(bf16[8,32,2048]{2,1,0:T(8,128)(2,1)S(1)} %pad_maximum_fusion.11), channel_id=1, source_target_pairs={{0,8},{1,9},{2,10},{3,11},{4,12},{5,13},{6,14},{7,15},{8,0},{9,1},... | collective-permute-start | bytes 3145736 | tf_op jit(solution)/shard_map/ppermute | solution.py:19
  346.6 42.1 %collective-permute-start.52 = (bf16[8,48,2048]{2,1,0:T(8,128)(2,1)S(1)}, bf16[8,48,2048]{2,1,0:T(8,128)(2,1)S(1)}, u32[]{:S(2)}, u32[]{:S(2)}) collective-permute-start(bf16[8,48,2048]{2,1,0:T(8,128)(2,1)S(1)} %pad_maximum_fusion.8), channel_id=1, source_target_pairs={{0,1},{1,0},{2,3},{3,2},{4,5},{5,4},{6,7},{7,6},{8,9},{9,8},{10,11... | collective-permute-start | bytes 4718600 | tf_op jit(solution)/shard_map/ppermute | solution.py:19
  363.5 51.3 %collective-permute-start.53 = (bf16[8,48,2048]{2,1,0:T(8,128)(2,1)S(1)}, bf16[8,48,2048]{2,1,0:T(8,128)(2,1)S(1)}, u32[]{:S(2)}, u32[]{:S(2)}) collective-permute-start(bf16[8,48,2048]{2,1,0:T(8,128)(2,1)S(1)} %pad_maximum_fusion.8), channel_id=1, source_target_pairs={{0,8},{1,9},{2,10},{3,11},{4,12},{5,13},{6,14},{7,15},{8,0},{9,1},... | collective-permute-start | bytes 4718600 | tf_op jit(solution)/shard_map/ppermute | solution.py:19
  366.4 38.0 %collective-permute-start.46 = (bf16[8,48,2048]{2,1,0:T(8,128)(2,1)S(1)}, bf16[8,48,2048]{2,1,0:T(8,128)(2,1)S(1)}, u32[]{:S(2)}, u32[]{:S(2)}) collective-permute-start(bf16[8,48,2048]{2,1,0:T(8,128)(2,1)S(1)} %pad_maximum_fusion.7), channel_id=1, source_target_pairs={{0,16},{1,17},{2,18},{3,19},{4,20},{5,21},{6,22},{7,23},{8,24},{9,... | collective-permute-start | bytes 4718600 | tf_op jit(solution)/shard_map/ppermute | solution.py:19
  383.9 54.1 %collective-permute-start.13 = (bf16[8,48,2048]{2,1,0:T(8,128)(2,1)S(1)}, bf16[8,48,2048]{2,1,0:T(8,128)(2,1)S(1)}, u32[]{:S(2)}, u32[]{:S(2)}) collective-permute-start(bf16[8,48,2048]{2,1,0:T(8,128)(2,1)S(1)} %pad_maximum_fusion.5), channel_id=1, source_target_pairs={{0,16},{1,17},{2,18},{3,19},{4,20},{5,21},{6,22},{7,23},{8,24},{9,... | collective-permute-start | bytes 4718600 | tf_op jit(solution)/shard_map/ppermute | solution.py:19
  388.7 51.6 %collective-permute-start.14 = (bf16[8,48,2048]{2,1,0:T(8,128)(2,1)S(1)}, bf16[8,48,2048]{2,1,0:T(8,128)(2,1)S(1)}, u32[]{:S(2)}, u32[]{:S(2)}) collective-permute-start(bf16[8,48,2048]{2,1,0:T(8,128)(2,1)S(1)} %pad_maximum_fusion.5), channel_id=1, source_target_pairs={{0,8},{1,9},{2,10},{3,11},{4,12},{5,13},{6,14},{7,15},{8,0},{9,1},... | collective-permute-start | bytes 4718600 | tf_op jit(solution)/shard_map/ppermute | solution.py:19
  485.3 94.3 %collective-permute-start.29 = (bf16[16,128,256]{2,1,0:T(8,128)(2,1)}, bf16[16,128,256]{2,1,0:T(8,128)(2,1)}, u32[]{:S(2)}, u32[]{:S(2)}) collective-permute-start(bf16[16,128,256]{2,1,0:T(8,128)(2,1)} %get-tuple-element.109), channel_id=1, source_target_pairs={{0,8},{1,9},{2,10},{3,11},{4,12},{5,13},{6,14},{7,15},{8,0},{9,1},... | collective-permute-start | bytes 3145736 | tf_op jit(solution)/shard_map/ppermute | solution.py:19
  510.4 69.2 %collective-permute-start.28 = (bf16[16,128,64]{2,1,0:T(8,128)(2,1)}, bf16[16,128,64]{2,1,0:T(8,128)(2,1)S(1)}, u32[]{:S(2)}, u32[]{:S(2)}) collective-permute-start(bf16[16,128,64]{2,1,0:T(8,128)(2,1)} %get-tuple-element.111), channel_id=1, source_target_pairs={{0,8},{1,9},{2,10},{3,11},{4,12},{5,13},{6,14},{7,15},{8,0},{9,1},... | collective-permute-start | bytes 786440 | tf_op jit(solution)/shard_map/ppermute | solution.py:19
  590.0 83.3 %collective-permute-start.31 = (bf16[8,48,2048]{2,1,0:T(8,128)(2,1)S(1)}, bf16[8,48,2048]{2,1,0:T(8,128)(2,1)S(1)}, u32[]{:S(2)}, u32[]{:S(2)}) collective-permute-start(bf16[8,48,2048]{2,1,0:T(8,128)(2,1)S(1)} %bitcast.304), channel_id=1, source_target_pairs={{0,16},{1,17},{2,18},{3,19},{4,20},{5,21},{6,22},{7,23},{8,24},{9,... | collective-permute-start | bytes 4718600 | tf_op jit(solution)/shard_map/ppermute | solution.py:19
  591.8 83.1 %collective-permute-start.35 = (bf16[8,48,2048]{2,1,0:T(8,128)(2,1)S(1)}, bf16[8,48,2048]{2,1,0:T(8,128)(2,1)S(1)}, u32[]{:S(2)}, u32[]{:S(2)}) collective-permute-start(bf16[8,48,2048]{2,1,0:T(8,128)(2,1)S(1)} %bitcast.302), channel_id=1, source_target_pairs={{0,1},{1,0},{2,3},{3,2},{4,5},{5,4},{6,7},{7,6},{8,9},{9,8},{10,11... | collective-permute-start | bytes 4718600 | tf_op jit(solution)/shard_map/ppermute | solution.py:19
  613.9 71.6 %collective-permute-start.64 = (bf16[8,48,2048]{2,1,0:T(8,128)(2,1)S(1)}, bf16[8,48,2048]{2,1,0:T(8,128)(2,1)S(1)}, u32[]{:S(2)}, u32[]{:S(2)}) collective-permute-start(bf16[8,48,2048]{2,1,0:T(8,128)(2,1)S(1)} %bitcast.305), channel_id=1, source_target_pairs={{0,16},{1,17},{2,18},{3,19},{4,20},{5,21},{6,22},{7,23},{8,24},{9,... | collective-permute-start | bytes 4718600 | tf_op jit(solution)/shard_map/ppermute | solution.py:19
  615.8 72.7 %collective-permute-start.68 = (bf16[8,48,2048]{2,1,0:T(8,128)(2,1)S(1)}, bf16[8,48,2048]{2,1,0:T(8,128)(2,1)S(1)}, u32[]{:S(2)}, u32[]{:S(2)}) collective-permute-start(bf16[8,48,2048]{2,1,0:T(8,128)(2,1)S(1)} %bitcast.303), channel_id=1, source_target_pairs={{0,1},{1,0},{2,3},{3,2},{4,5},{5,4},{6,7},{7,6},{8,9},{9,8},{10,11... | collective-permute-start | bytes 4718600 | tf_op jit(solution)/shard_map/ppermute | solution.py:19
  674.9 53.4 %collective-permute-start.32 = (bf16[4,48,2048]{2,1,0:T(8,128)(2,1)S(1)}, bf16[4,48,2048]{2,1,0:T(8,128)(2,1)S(1)}, u32[]{:S(2)}, u32[]{:S(2)}) collective-permute-start(bf16[4,48,2048]{2,1,0:T(8,128)(2,1)S(1)} %slice.523), channel_id=1, source_target_pairs={{0,1},{1,0},{2,3},{3,2},{4,5},{5,4},{6,7},{7,6},{8,9},{9,8},{10,11... | collective-permute-start | bytes 2359304 | tf_op jit(solution)/shard_map/ppermute | solution.py:19
  684.4 47.6 %collective-permute-start.36 = (bf16[4,48,2048]{2,1,0:T(8,128)(2,1)S(1)}, bf16[4,48,2048]{2,1,0:T(8,128)(2,1)S(1)}, u32[]{:S(2)}, u32[]{:S(2)}) collective-permute-start(bf16[4,48,2048]{2,1,0:T(8,128)(2,1)S(1)} %slice.531), channel_id=1, source_target_pairs={{0,2},{1,3},{2,0},{3,1},{4,6},{5,7},{6,4},{7,5},{8,10},{9,11},{10,... | collective-permute-start | bytes 2359304 | tf_op jit(solution)/shard_map/ppermute | solution.py:19
  688.4 45.4 %collective-permute-start.65 = (bf16[4,48,2048]{2,1,0:T(8,128)(2,1)S(1)}, bf16[4,48,2048]{2,1,0:T(8,128)(2,1)S(1)}, u32[]{:S(2)}, u32[]{:S(2)}) collective-permute-start(bf16[4,48,2048]{2,1,0:T(8,128)(2,1)S(1)} %slice.558), channel_id=1, source_target_pairs={{0,1},{1,0},{2,3},{3,2},{4,5},{5,4},{6,7},{7,6},{8,9},{9,8},{10,11... | collective-permute-start | bytes 2359304 | tf_op jit(solution)/shard_map/ppermute | solution.py:19
  689.2 45.1 %collective-permute-start.69 = (bf16[4,48,2048]{2,1,0:T(8,128)(2,1)S(1)}, bf16[4,48,2048]{2,1,0:T(8,128)(2,1)S(1)}, u32[]{:S(2)}, u32[]{:S(2)}) collective-permute-start(bf16[4,48,2048]{2,1,0:T(8,128)(2,1)S(1)} %slice.566), channel_id=1, source_target_pairs={{0,2},{1,3},{2,0},{3,1},{4,6},{5,7},{6,4},{7,5},{8,10},{9,11},{10,... | collective-permute-start | bytes 2359304 | tf_op jit(solution)/shard_map/ppermute | solution.py:19
  (129 other events, 2186.7 us)

commit v2 on v1

v2 whole, which is shorter than its diff:
```python
import jax
import jax.numpy as jnp
from jax import lax
from jax.experimental import pallas as pl
from jax.experimental.pallas import tpu as pltpu
from jax.sharding import PartitionSpec as P

HEAD_DIM = 64
ROT = 32
AXES = ("head", "blk")
GROUP = 16
CHUNK = 512
NEG = -1e30
OWN_GATHER = False
OWN_REDUCE = False
F32 = jnp.float32
BF16 = jnp.bfloat16


def swap(block, mask, count):
    return lax.ppermute(block, AXES, [(i, i ^ mask) for i in range(count)])


def dot_nn(a, b):
    return lax.dot_general(a, b, (((1,), (0,)), ((), ())), preferred_element_type=F32)


def dot_nt(a, b):
    return lax.dot_general(a, b, (((1,), (1,)), ((), ())), preferred_element_type=F32)


def dot_tn(a, b):
    return lax.dot_general(a, b, (((0,), (0,)), ((), ())), preferred_element_type=F32)


def opening_of(packed, lengths):
    starts = jnp.cumsum(lengths) - lengths
    inside = packed[..., None] >= starts
    return jnp.max(jnp.where(inside, starts, 0), axis=-1)


def pieces_of(blks, rows, own):
    bits = [1 << i for i in range(blks.bit_length() - 1)][::-1]
    if not own:
        return [((0, rows), bits)]
    half = rows // 2
    if blks == 8:
        z2, z1, y = bits
        return [((0, half), [z2, z1, y]), ((half, rows), [z2, y, z1])]
    return [((0, half), bits), ((half, rows), bits[1:] + bits[:1])]


def slot_masks(order):
    masks = [0]
    for mask in order:
        masks = masks + [m ^ mask for m in masks]
    return masks


def prepare_kernel(z_ref, bias_ref, cos_ref, up_ref, down_ref, out_ref):
    heads = out_ref.shape[0]
    span = heads * HEAD_DIM
    z = z_ref[...] + bias_ref[...]
    lanes = cos_ref.shape[1]
    half = ROT // 2
    turned = []
    for first in range(0, 2 * span, lanes):
        u = z[:, first : first + lanes]
        turned.append(
            u * cos_ref[...]
            + pltpu.roll(u, lanes - half, 1) * up_ref[...]
            + pltpu.roll(u, half, 1) * down_ref[...]
        )
    both = jnp.concatenate(turned, axis=1)
    for r in range(heads):
        a, b = r * HEAD_DIM, (r + 1) * HEAD_DIM
        row = [both[:, a:b], both[:, span + a : span + b], z[:, 2 * span + a : 2 * span + b]]
        out_ref[r] = jnp.concatenate(row, axis=1).astype(BF16)


def prepare(z, bias, place, heads):
    rows, width = z.shape
    lanes = 2 * HEAD_DIM
    block = min(256, rows)
    lane = jnp.arange(lanes, dtype=jnp.int32) % HEAD_DIM
    half = ROT // 2
    frequency = 10000.0 ** (-2.0 * (lane % half).astype(F32) / ROT)
    angles = place.astype(F32)[:, None] * frequency[None, :]
    cosine = jnp.where(lane < ROT, jnp.cos(angles), 1.0)
    sine = jnp.sin(angles)
    up = jnp.where(lane < half, -sine, 0.0)
    down = jnp.where((lane >= half) & (lane < ROT), sine, 0.0)
    table = pl.BlockSpec((block, lanes), lambda i: (i, 0))
    return pl.pallas_call(
        prepare_kernel,
        out_shape=jax.ShapeDtypeStruct((heads, rows, 3 * HEAD_DIM), BF16),
        grid=(rows // block,),
        in_specs=[
            pl.BlockSpec((block, width), lambda i: (i, 0)),
            pl.BlockSpec((1, width), lambda i: (0, 0)),
            table, table, table,
        ],
        out_specs=pl.BlockSpec((heads, block, 3 * HEAD_DIM), lambda i: (0, i, 0)),
        compiler_params=pltpu.CompilerParams(vmem_limit_bytes=32 * 1024 * 1024),
        cost_estimate=pl.CostEstimate(
            flops=rows * width * 8, bytes_accessed=rows * width * 8, transcendentals=0
        ),
        name="rotary",
    )(z, bias, cosine, up, down)


def rope_t(u, cosine, sine):
    half = ROT // 2
    top, low = u[:half], u[half:ROT]
    return jnp.concatenate(
        [top * cosine - low * sine, low * cosine + top * sine, u[ROT:]], axis=0
    )


def rows_of(refs, at=slice(None)):
    found = []
    for ref in refs:
        block = ref[:, at, :]
        found.append(block.reshape(block.shape[0] * block.shape[1], block.shape[2]))
    return jnp.concatenate(found, axis=0)


def forward_kernel(sources, *refs):
    lo_ref, mid_ref = refs[:2]
    in_refs = refs[2 : 2 + sources]
    pq_ref, lq_ref, kp_ref = refs[2 + sources : 5 + sources]
    att_refs = refs[5 + sources : 5 + 2 * sources]
    ot_ref, lse_ref, q_ref, k_ref, v_ref, qt_ref, kt_ref, vt_ref = refs[5 + 2 * sources :]
    t = pl.program_id(0)
    chunk = q_ref.shape[1]
    rows = rows_of(in_refs)
    per = rows.shape[0] // chunk
    for c in range(per):
        index = t * per + c
        part = rows[c * chunk : (c + 1) * chunk]
        q_ref[index] = part[:, :HEAD_DIM]
        k_ref[index] = part[:, HEAD_DIM : 2 * HEAD_DIM]
        v_ref[index] = part[:, 2 * HEAD_DIM :]
        turned = part.astype(F32).T
        qt_ref[index] = (turned[:HEAD_DIM] * HEAD_DIM**-0.5).astype(BF16)
        kt_ref[index] = turned[HEAD_DIM : 2 * HEAD_DIM].astype(BF16)
        vt_ref[index] = turned[2 * HEAD_DIM :].astype(BF16)
    outs = []
    for c in range(per):
        qt = qt_ref[t * per + c]
        query_pos, query_lo = pq_ref[c], lq_ref[c]

        def step(kc, state, masked):
            run_max, run_sum, acc = state
            scores = dot_nn(k_ref[kc], qt)
            if masked:
                key_pos = kp_ref[kc]
                visible = (key_pos <= query_pos) & (key_pos >= query_lo)
                scores = jnp.where(visible, scores, NEG)
            new_max = jnp.maximum(run_max, jnp.max(scores, axis=0, keepdims=True))
            weights = jnp.exp(scores - new_max)
            if masked:
                weights = jnp.where(visible, weights, 0.0)
            rescale = jnp.exp(run_max - new_max)
            run_sum = run_sum * rescale + jnp.sum(weights, axis=0, keepdims=True)
            acc = acc * rescale + dot_nn(vt_ref[kc], weights.astype(BF16))
            return new_max, run_sum, acc

        state = (
            jnp.full((1, chunk), NEG, F32),
            jnp.zeros((1, chunk), F32),
            jnp.zeros((HEAD_DIM, chunk), F32),
        )
        state = lax.fori_loop(lo_ref[t], mid_ref[t], lambda i, s: step(i, s, True), state)
        state = lax.fori_loop(mid_ref[t], t * per, lambda i, s: step(i, s, False), state)
        state = lax.fori_loop(t * per, (t + 1) * per, lambda i, s: step(i, s, True), state)
        run_max, run_sum, acc = state
        out = acc / run_sum
        ot_ref[c] = out
        lse_ref[c] = run_max + jnp.log(run_sum)
        outs.append(out.T.astype(BF16))
    att = outs[0] if per == 1 else jnp.concatenate(outs, axis=0)
    span = att.shape[0] // sources
    for i, ref in enumerate(att_refs):
        ref[...] = att[i * span : (i + 1) * span].reshape(ref.shape)


def backward_kernel(sources, *refs):
    lo_ref, mid_ref = refs[:2]
    g_refs = refs[2 : 2 + sources]
    cos_ref, sin_ref, pq_ref, lq_ref, kp_ref, ot_ref, lse_ref = refs[2 + sources : 9 + sources]
    q_ref, k_ref, v_ref, qt_ref, kt_ref = refs[9 + sources : 14 + sources]
    out_refs = refs[14 + sources : 14 + 2 * sources]
    dk_ref, dv_ref = refs[14 + 2 * sources :]
    t = pl.program_id(0)
    chunk = q_ref.shape[1]
    scaling = HEAD_DIM**-0.5
    grads = rows_of(g_refs)
    per = grads.shape[0] // chunk
    for c in range(per):
        dk_ref[t * per + c] = jnp.zeros((chunk, HEAD_DIM), F32)
        dv_ref[t * per + c] = jnp.zeros((chunk, HEAD_DIM), F32)
    parts = []
    for c in range(per):
        index = t * per + c
        do = grads[c * chunk : (c + 1) * chunk]
        dot32 = do.astype(F32).T
        dot16 = dot32.astype(BF16)
        delta = jnp.sum(dot32 * ot_ref[c], axis=0, keepdims=True)
        lse = lse_ref[c]
        q, qt = q_ref[index], qt_ref[index]
        query_pos, query_lo = pq_ref[c], lq_ref[c]

        def step(kc, dqt, masked):
            probs = jnp.exp(dot_nn(k_ref[kc], qt) - lse)
            if masked:
                key_pos = kp_ref[kc]
                visible = (key_pos <= query_pos) & (key_pos >= query_lo)
                probs = jnp.where(visible, probs, 0.0)
            dv_ref[kc] += dot_nn(probs.astype(BF16), do)
            prob_grad = dot_nn(v_ref[kc], dot16)
            score_grad = (probs * (prob_grad - delta)).astype(BF16)
            dk_ref[kc] += dot_nn(score_grad, q)
            return dqt + dot_nn(kt_ref[kc], score_grad)

        dqt = jnp.zeros((HEAD_DIM, chunk), F32)
        dqt = lax.fori_loop(lo_ref[t], mid_ref[t], lambda i, s: step(i, s, True), dqt)
        dqt = lax.fori_loop(mid_ref[t], t * per, lambda i, s: step(i, s, False), dqt)
        dqt = lax.fori_loop(t * per, (t + 1) * per, lambda i, s: step(i, s, True), dqt)
        parts.append(rope_t(dqt * scaling, cos_ref[index], -sin_ref[index]).T)

    def store(block, u, first):
        span = block.shape[0] // sources
        here = pl.ds(pl.multiple_of(u * GROUP, GROUP), GROUP)
        for i, ref in enumerate(out_refs):
            part = block[i * span : (i + 1) * span].astype(BF16)
            part = part.reshape(ref.shape[0], GROUP, part.shape[1])
            ref[:, here, first : first + part.shape[2]] = part

    store(parts[0] if per == 1 else jnp.concatenate(parts, axis=0), t, 0)

    @pl.when(t == pl.num_programs(0) - 1)
    def _():
        def finish(u, carry):
            found = []
            for c in range(per):
                index = u * per + c
                dkt = rope_t(dk_ref[index].T * scaling, cos_ref[index], -sin_ref[index])
                found.append(jnp.concatenate([dkt.T, dv_ref[index]], axis=1))
            store(found[0] if per == 1 else jnp.concatenate(found, axis=0), u, HEAD_DIM)
            return carry

        lax.fori_loop(0, pl.num_programs(0), finish, 0)


def whole_block(shape):
    zeros = (0,) * len(shape)
    return pl.BlockSpec(tuple(shape), lambda t, *refs: zeros)


def tile_block(shape, axis):
    def place(t, *refs):
        return tuple(t if i == axis else 0 for i in range(len(shape)))

    return pl.BlockSpec(tuple(shape), place)


def attention_meta(positions, seq_lengths, chunk):
    tiles, tile = positions.shape
    count = tiles * tile // chunk
    per = tile // chunk
    opening = opening_of(positions, seq_lengths)
    frequency = 10000.0 ** (-2.0 * jnp.arange(ROT // 2, dtype=F32) / ROT)
    angles = (positions - opening).astype(F32).reshape(count, 1, chunk) * frequency[None, :, None]
    ends = jnp.arange(tiles, dtype=jnp.int32) * tile
    first_open = opening_of(ends, seq_lengths)
    last_open = opening_of(ends + tile - 1, seq_lengths)
    own = jnp.arange(tiles, dtype=jnp.int32) * per
    low = (first_open // tile) * per
    middle = jnp.minimum(((last_open + tile - 1) // tile) * per, own)
    return dict(
        low=low.astype(jnp.int32),
        middle=middle.astype(jnp.int32),
        cosine=jnp.cos(angles),
        sine=jnp.sin(angles),
        query_pos=positions.reshape(count, 1, chunk),
        query_lo=opening.reshape(count, 1, chunk),
        key_pos=positions.reshape(count, chunk, 1),
    )


def attention_forward(parts, meta):
    sources = len(parts)
    slots, rows, width = parts[0].shape
    tile = sources * slots * GROUP
    tiles = rows // GROUP
    count, _, chunk = meta["query_pos"].shape
    per = tile // chunk
    nat = jax.ShapeDtypeStruct((count, chunk, HEAD_DIM), BF16)
    turned = jax.ShapeDtypeStruct((count, HEAD_DIM, chunk), BF16)
    out = jax.ShapeDtypeStruct((slots, rows, HEAD_DIM), BF16)
    found = pl.pallas_call(
        lambda *refs: forward_kernel(sources, *refs),
        out_shape=[out] * sources
        + [
            jax.ShapeDtypeStruct((count, HEAD_DIM, chunk), F32),
            jax.ShapeDtypeStruct((count, 1, chunk), F32),
            nat, nat, nat, turned, turned,
        ],
        grid_spec=pltpu.PrefetchScalarGridSpec(
            num_scalar_prefetch=2,
            grid=(tiles,),
            in_specs=[tile_block((slots, GROUP, width), 1)] * sources
            + [
                tile_block((per, 1, chunk), 0),
                tile_block((per, 1, chunk), 0),
                whole_block((count, chunk, 1)),
            ],
            out_specs=[tile_block((slots, GROUP, HEAD_DIM), 1)] * sources
            + [
                tile_block((per, HEAD_DIM, chunk), 0),
                tile_block((per, 1, chunk), 0),
                whole_block(nat.shape),
                whole_block(nat.shape),
                whole_block(nat.shape),
                whole_block(turned.shape),
                whole_block(turned.shape),
            ],
            scratch_shapes=[pltpu.VMEM(turned.shape, BF16)],
        ),
        compiler_params=pltpu.CompilerParams(
            dimension_semantics=("arbitrary",), vmem_limit_bytes=58 * 1024 * 1024
        ),
        cost_estimate=pl.CostEstimate(
            flops=20_000_000_000, bytes_accessed=12_000_000, transcendentals=6_000_000
        ),
        name="attention_forward",
    )(
        meta["low"], meta["middle"], *parts,
        meta["query_pos"], meta["query_lo"], meta["key_pos"],
    )
    return found[:sources], found[sources:]


def attention_backward(grads, meta, saved):
    sources = len(grads)
    slots, rows, _ = grads[0].shape
    tile = sources * slots * GROUP
    tiles = rows // GROUP
    count, _, chunk = meta["query_pos"].shape
    per = tile // chunk
    half = ROT // 2
    out = jax.ShapeDtypeStruct((slots, rows, 3 * HEAD_DIM), BF16)
    ot, lse, q, k, v, qt, kt = saved
    return pl.pallas_call(
        lambda *refs: backward_kernel(sources, *refs),
        out_shape=[out] * sources,
        grid_spec=pltpu.PrefetchScalarGridSpec(
            num_scalar_prefetch=2,
            grid=(tiles,),
            in_specs=[tile_block((slots, GROUP, HEAD_DIM), 1)] * sources
            + [
                whole_block((count, half, chunk)),
                whole_block((count, half, chunk)),
                tile_block((per, 1, chunk), 0),
                tile_block((per, 1, chunk), 0),
                whole_block((count, chunk, 1)),
                tile_block((per, HEAD_DIM, chunk), 0),
                tile_block((per, 1, chunk), 0),
                whole_block(q.shape),
                whole_block(k.shape),
                whole_block(v.shape),
                whole_block(qt.shape),
                whole_block(kt.shape),
            ],
            out_specs=[whole_block(out.shape)] * sources,
            scratch_shapes=[
                pltpu.VMEM((count, chunk, HEAD_DIM), F32),
                pltpu.VMEM((count, chunk, HEAD_DIM), F32),
            ],
        ),
        compiler_params=pltpu.CompilerParams(
            dimension_semantics=("arbitrary",), vmem_limit_bytes=62 * 1024 * 1024
        ),
        cost_estimate=pl.CostEstimate(
            flops=20_000_000_000, bytes_accessed=12_000_000, transcendentals=6_000_000
        ),
        name="attention_backward",
    )(
        meta["low"], meta["middle"], *grads, meta["cosine"], meta["sine"],
        meta["query_pos"], meta["query_lo"], meta["key_pos"], ot, lse, q, k, v, qt, kt,
    )


def gather_rows(rows, pieces, count, own):
    if not own:
        return lax.all_gather(rows, "blk", axis=0, tiled=False)
    found = []
    for (begin, end), order in pieces:
        held = rows[begin:end][None]
        for mask in order:
            held = jnp.concatenate([held, swap(held, mask, count)], axis=0)
        found.append(held)
    return jnp.concatenate(found, axis=1)


def reduce_rows(product, pieces, count, own):
    if not own:
        total = product(slice(None), slice(None)).astype(BF16)
        return lax.psum_scatter(total, "blk", scatter_dimension=0, tiled=False).astype(F32)
    found = []
    for (begin, end), order in pieces:
        middle = (1 << len(order)) // 2
        here = slice(begin, end)
        sent = product(slice(middle, None), here).astype(BF16)
        kept = product(slice(0, middle), here).astype(BF16)
        for mask in order[::-1][:-1]:
            total = kept.astype(F32) + swap(sent, mask, count).astype(F32)
            middle = middle // 2
            sent, kept = total[middle:].astype(BF16), total[:middle].astype(BF16)
        total = kept.astype(F32) + swap(sent, order[0], count).astype(F32)
        found.append(total[0])
    return jnp.concatenate(found, axis=0)


def gather_small(block, stages, count):
    for masks in stages:
        block = jnp.stack([block if m == 0 else swap(block, m, count) for m in masks])
    return block.reshape((-1,) + block.shape[len(stages) :])


def reduce_small(block, stages, count):
    for masks in stages[::-1]:
        block = block.reshape((len(masks), -1) + block.shape[1:])
        total = block[0]
        for i, m in enumerate(masks):
            if m:
                total = total + swap(block[i], m, count)
        block = total
    return block[0]


def exchange(parts, masks, count):
    return [part if m == 0 else swap(part, m, count) for part, m in zip(parts, masks)]


def gather_heads(block, masks, count):
    held = block[None]
    step = 1
    while step < len(masks):
        held = jnp.concatenate([held, swap(held, masks[step], count)], axis=0)
        step *= 2
    return held


def reduce_heads(product, masks, count):
    half = len(masks) // 2
    sent = product(range(half, 2 * half)).astype(BF16)
    total = product(range(half)) + swap(sent, masks[half], count).astype(F32)
    while half > 1:
        half //= 2
        sent = total[half:].astype(BF16)
        total = total[:half] + swap(sent, masks[half], count).astype(F32)
    return total[0]


def gelu_tanh(values):
    return jax.nn.gelu(values, approximate=True)


def gelu_back(hidden, act_grad):
    _, pullback = jax.vjp(gelu_tanh, hidden)
    return pullback(act_grad)[0]


def per_device(
    layer_in, out_grad, norm_gain, norm_bias, w_qkv, b_qkv, w_out, b_out, w_up, b_up,
    w_down, b_down, seq_lengths, token_place,
):
    heads, blks = lax.axis_size("head"), lax.axis_size("blk")
    count = heads * blks
    my_head, my_blk = lax.axis_index("head"), lax.axis_index("blk")
    me = my_head * blks + my_blk
    rows, width = layer_in.shape
    features = w_qkv.shape[1]
    units = w_up.shape[0]
    owners = HEAD_DIM // features
    member = me % owners
    own_gather = OWN_GATHER
    own_reduce = OWN_REDUCE
    relative = own_gather or own_reduce
    pieces = pieces_of(blks, rows, relative)
    head_bits = [blks << i for i in range(heads.bit_length() - 1)][::-1]
    head_masks = slot_masks(head_bits)
    stages = [list(range(blks)), [r * blks for r in range(heads)]]
    numbers = jnp.arange(count, dtype=jnp.int32)

    place = token_place.reshape(count, rows)
    ranks = place // count
    row_numbers = jnp.arange(rows, dtype=jnp.int32)
    own_ranks = lax.dynamic_slice_in_dim(ranks, me, 1, 0)
    order_hot = (own_ranks == row_numbers[:, None]).astype(BF16)
    x_sorted = dot_nn(order_hot, layer_in).astype(BF16)
    g_sorted = dot_nn(order_hot, out_grad).astype(BF16)
    x_all = gather_rows(x_sorted, pieces, count, own_gather).reshape(blks * rows, width)
    g_all = gather_rows(g_sorted, pieces, count, own_gather).reshape(blks * rows, width)

    vectors = jnp.stack([norm_gain, norm_bias, b_out, b_down])
    vectors = gather_small(vectors, stages, count)
    absolute = me ^ numbers
    choose = (absolute[None, :] == numbers[:, None]).astype(BF16)
    vectors = dot_nn(choose, vectors.reshape(count, -1)).reshape(count, 4, -1)
    vectors = jnp.transpose(vectors, (1, 0, 2)).reshape(4, width)
    gain, offset, out_bias, down_bias = (vectors[i][None] for i in range(4))

    qkv_full, out_full = w_qkv, w_out
    bias_full = b_qkv
    if owners > 1:
        order = member ^ jnp.arange(owners, dtype=jnp.int32)

        def of_owners(block):
            found = [block] + [swap(block, e, count) for e in range(1, owners)]
            return jnp.stack(found)[order]

        qkv_full = jnp.moveaxis(of_owners(w_qkv), 0, 1).reshape(3, HEAD_DIM, width)
        bias_full = jnp.moveaxis(of_owners(b_qkv), 0, 1).reshape(3, HEAD_DIM)
        out_full = of_owners(w_out).reshape(HEAD_DIM, width)
    qkv_heads = gather_heads(qkv_full.reshape(3 * HEAD_DIM, width), head_masks, count)
    up_heads = gather_heads(w_up, head_masks, count).reshape(heads * units, width)
    out_heads = gather_heads(out_full, head_masks, count)
    down_heads = gather_heads(w_down, head_masks, count).reshape(heads * units, width)
    biases = gather_heads(jnp.concatenate([bias_full.reshape(-1), b_up]), head_masks, count)
    qkv_heads = qkv_heads.reshape(heads, 3, HEAD_DIM, width)
    qkv_rows = jnp.swapaxes(qkv_heads, 0, 1).reshape(3 * heads * HEAD_DIM, width)
    qkv_bias = biases[:, : 3 * HEAD_DIM].reshape(heads, 3, HEAD_DIM).astype(F32)
    qkv_bias = jnp.swapaxes(qkv_bias, 0, 1).reshape(1, -1)
    up_bias = biases[:, 3 * HEAD_DIM :].reshape(1, -1).astype(F32)

    sorted_place = jnp.sum(
        jnp.where(ranks[:, None, :] == row_numbers[None, :, None], place[:, None, :], 0), axis=2
    )
    found = []
    for (begin, end), order in pieces:
        masks = jnp.array(slot_masks(order), dtype=jnp.int32)
        slot_blk = (my_blk ^ masks) if relative else jnp.arange(blks, dtype=jnp.int32)
        slot_head = my_head ^ jnp.array([m // blks for m in head_masks], dtype=jnp.int32)
        device = (slot_head[:, None] * blks + slot_blk[None, :]).reshape(-1)
        part = sorted_place[:, begin:end]
        chosen = jnp.where((device[:, None] == numbers[None, :])[:, :, None], part[None], 0)
        found.append(jnp.sum(chosen, axis=1))
    positions = jnp.concatenate(found, axis=1)
    own_positions = positions[:blks].reshape(-1)
    own_place = own_positions - opening_of(own_positions, seq_lengths)
    tiles = rows // GROUP
    positions = jnp.transpose(positions.reshape(count, tiles, GROUP), (1, 0, 2))
    positions = positions.reshape(tiles, count * GROUP)
    meta = attention_meta(positions, seq_lengths, min(CHUNK, count * GROUP))

    def normalize(values):
        values = values.astype(F32)
        center = jnp.mean(values, axis=-1, keepdims=True)
        centered = values - center
        variance = jnp.mean(centered * centered, axis=-1, keepdims=True)
        inverse = lax.rsqrt(variance + 1e-05)
        return centered * inverse, inverse

    normed = (normalize(x_all)[0] * gain + offset).astype(BF16)
    qkv = prepare(dot_nt(normed, qkv_rows), qkv_bias, own_place, heads)
    qkv = [qkv[r].reshape(blks, rows, 3 * HEAD_DIM) for r in range(heads)]
    attended, saved = attention_forward(exchange(qkv, head_masks, count), meta)
    attended = exchange(attended, head_masks, count)
    hidden = dot_nt(normed, up_heads) + up_bias
    active = gelu_tanh(hidden).astype(BF16)

    def own_features(parts, kinds):
        if owners == 1:
            return jnp.concatenate(parts, axis=2)
        found = []
        for part in parts:
            split = part.reshape(blks, rows, kinds, owners, features)
            found.append(lax.dynamic_index_in_dim(split, member, 3, False).reshape(blks, rows, -1))
        return jnp.concatenate(found, axis=2)

    att = own_features(attended, 1)
    out_own = out_heads if owners == 1 else gather_heads(w_out, head_masks, count)
    out_own = out_own.reshape(heads * features, width)
    act = active.reshape(blks, rows, heads * units)

    def flat(block):
        return block.reshape(-1, block.shape[-1])

    def mixed_part(slots, here):
        total = dot_nn(flat(att[slots, here]), out_own)
        total = total + dot_nn(flat(act[slots, here]), down_heads)
        return total.reshape(-1, (rows if here == slice(None) else here.stop - here.start), width)

    mixed = reduce_rows(mixed_part, pieces, count, own_reduce)

    heads_grad = dot_nt(g_all, out_heads.reshape(heads * HEAD_DIM, width)).astype(BF16)
    heads_grad = [
        heads_grad[:, r * HEAD_DIM : (r + 1) * HEAD_DIM].reshape(blks, rows, HEAD_DIM)
        for r in range(heads)
    ]
    qkv_grad = attention_backward(exchange(heads_grad, head_masks, count), meta, saved)
    qkv_grad = own_features(exchange(qkv_grad, head_masks, count), 3)
    hidden_grad = gelu_back(hidden, dot_nt(g_all, down_heads)).astype(BF16)
    hid_grad = hidden_grad.reshape(blks, rows, heads * units)
    qkv_own = qkv_heads if owners == 1 else gather_heads(w_qkv, head_masks, count)
    qkv_own = qkv_own.reshape(heads * 3 * features, width)

    def normed_part(slots, here):
        total = dot_nn(flat(qkv_grad[slots, here]), qkv_own)
        total = total + dot_nn(flat(hid_grad[slots, here]), up_heads)
        return total.reshape(-1, (rows if here == slice(None) else here.stop - here.start), width)

    normed_grad = reduce_rows(normed_part, pieces, count, own_reduce)

    def weight_grads(left, right, per_owner):
        def product(which):
            split = left.reshape(-1, heads, per_owner)
            chosen = jnp.concatenate([split[:, o] for o in which], axis=1)
            return dot_tn(chosen, right).reshape(len(which), per_owner, width)

        return reduce_heads(product, head_masks, count)

    w_down_grad = weight_grads(active, g_all, units)
    w_out_grad = weight_grads(flat(att), g_all, features)
    w_up_grad = weight_grads(hidden_grad, normed, units)
    w_qkv_grad = weight_grads(flat(qkv_grad), normed, 3 * features)
    b_parts = jnp.concatenate(
        [
            jnp.sum(flat(qkv_grad).astype(F32), axis=0).reshape(heads, -1),
            jnp.sum(hidden_grad.astype(F32), axis=0).reshape(heads, -1),
        ],
        axis=1,
    )
    b_grads = sum(exchange([b_parts[r] for r in range(heads)], head_masks, count))

    own_x = x_sorted.astype(F32)
    layer_out = (own_x + mixed + out_bias + down_bias).astype(BF16)
    layer_out = dot_tn(order_hot, layer_out).astype(BF16)
    x_hat, inverse = normalize(x_sorted)
    e = normed_grad * gain
    input_part = inverse * (
        e
        - jnp.mean(e, axis=-1, keepdims=True)
        - x_hat * jnp.mean(e * x_hat, axis=-1, keepdims=True)
    )
    input_grad = (g_sorted.astype(F32) + input_part).astype(BF16)
    input_grad = dot_tn(order_hot, input_grad).astype(BF16)
    sums = jnp.stack(
        [
            jnp.sum(normed_grad * x_hat, axis=0),
            jnp.sum(normed_grad, axis=0),
            jnp.sum(g_sorted.astype(F32), axis=0),
        ]
    )
    chosen = (absolute[:, None] == numbers[None, :]).astype(F32)
    sums = lax.dot_general(
        chosen,
        jnp.transpose(sums.reshape(3, count, -1), (1, 0, 2)).reshape(count, -1),
        (((1,), (0,)), ((), ())),
        precision=lax.Precision.HIGHEST,
        preferred_element_type=F32,
    ).reshape(count, 3, -1)
    sums = reduce_small(sums, stages, count)
    return (
        layer_out,
        input_grad,
        sums[0],
        sums[1],
        w_qkv_grad.reshape(3, features, width),
        b_grads[: 3 * features].reshape(3, features),
        w_out_grad,
        sums[2],
        w_up_grad,
        b_grads[3 * features :],
        w_down_grad,
        sums[2],
    )


def solution(mesh):
    rows, vector = P(AXES, None), P(AXES)
    qkv, qkv_bias = P(None, AXES, None), P(None, AXES)
    in_specs = (
        rows, rows, vector, vector, qkv, qkv_bias, rows, vector, rows, vector, rows, vector,
        P(), P(),
    )
    out_specs = (
        rows, rows, vector, vector, qkv, qkv_bias, rows, vector, rows, vector, rows, vector,
    )
    return jax.shard_map(
        per_device, mesh=mesh, in_specs=in_specs, out_specs=out_specs, check_vma=False
    )
```

time: 807 us -> 454 us (0.56)
  local copies, waits for them, and re-layouts: 269 us -> 30.5 us
  waiting for transfers between devices: 234 us -> 152 us
  starting transfers between devices: 103 us -> 51.5 us
  other arithmetic: 40.3 us -> 57.3 us
  between operations: 2.65 us -> 15 us
  matrix products: 103 us -> 90.8 us
    gather x385 -> x0, local copies, waits for them, and re-layouts: 192 us -> none
    ppermute x86 -> x53, waiting for transfers between devices: 234 us -> 140 us  [swap(): return lax.ppermute(block, AXES, [(i, i ^ mask) for i in range(count)])]
    ppermute x86 -> x53, starting transfers between devices: 103 us -> 51.1 us  [swap(): return lax.ppermute(block, AXES, [(i, i ^ mask) for i in range(count)])]
    dot_general x24 -> x4, matrix products: 52.6 us -> 23.6 us  [dot_nt(): lax.dot_general(a, b, (((1,), (1,)), ((), ())), preferred_element_type=F32)]
    slice x35 -> x13, local copies, waits for them, and re-layouts: 30 us -> 4.02 us  [the longest x5 1.38 us: per_device(): heads_grad[:, r * HEAD_DIM:(r + 1) * HEAD_DIM].reshape(blks, rows, HEAD_DIM)]
    unnamed x178 -> x92, local copies, waits for them, and re-layouts: 30.9 us -> 5.54 us
    concatenate x24 -> x21, other arithmetic: 13.7 us -> 29.4 us  [the longest x10 22.8 us: gather_heads(): held = jnp.concatenate([held, swap(held, masks[step], count)], axis=0)]
    all_gather x0 -> x2, waiting for transfers between devices: none -> 11.8 us  [gather_rows(): return lax.all_gather(rows, 'blk', axis=0, tiled=False)]
  transfers between devices with their start and end apart: 86 -> 57, of which waited for: 27 -> 19; matrix products, arithmetic and copies ran while one was open for 49% -> 36% of each run, Pallas kernels for 6% -> 6%
where the time goes in v2:
time: 454 us; the launch traced here: 448 us
  waiting for transfers between devices  152 us (33%)
  matrix products  90.8 us (20%)
  other arithmetic  57.3 us (13%)
  starting transfers between devices  51.5 us (11%)
  Pallas kernels  50.3 us (11%)
  local copies, waits for them, and re-layouts  30.5 us (7%)
  between operations  15 us (3%)
    ppermute x53, waiting for transfers between devices, swap(): return lax.ppermute(block, AXES, [(i, i ^ mask) for i in range(count)])  140 us
    ppermute x53, starting transfers between devices, swap(): return lax.ppermute(block, AXES, [(i, i ^ mask) for i in range(count)])  51.1 us
    dot_general x10, matrix products, dot_tn(): lax.dot_general(a, b, (((0,), (0,)), ((), ())), preferred_element_type=F32)  35.2 us
    dot_general x7, matrix products, dot_nn(): lax.dot_general(a, b, (((1,), (0,)), ((), ())), preferred_element_type=F32)  31.7 us
    pallas_call x1, Pallas kernels, attention_backward(): pl.pallas_call(lambda *refs: backward_kernel(sources, *refs), out_shape=[...  25.5 us
    dot_general x4, matrix products, dot_nt(): lax.dot_general(a, b, (((1,), (1,)), ((), ())), preferred_element_type=F32)  23.6 us
    concatenate x10, other arithmetic, gather_heads(): held = jnp.concatenate([held, swap(held, masks[step], count)], axis=0)  22.8 us
    pallas_call x1, Pallas kernels, attention_forward(): pl.pallas_call(lambda *refs: forward_kernel(sources, *refs), out_shape=[o...  22.5 us
  transfers between devices with their start and end apart: 57, of which 19 were waited for; matrix products, arithmetic and copies ran while one was open for 36% of the time, Pallas kernels for 6%

profile of v2, /device:TPU:0, one launch (start us, length us, event | category | flops | bytes accessed | tf_op | source)
XLA Modules:
  0.0 447.6 jit_solution(3188464580031671927)
XLA Ops:
  33.5 3.6 collective-permute-start.5
  41.4 44.7 %collective-permute-done.12 = bf16[1,448]{1,0:T(2,128)(2,1)S(1)} collective-permute-done((bf16[1,448]{1,0:T(2,128)(2,1)S(1)}, bf16[1,448]{1,0:T(2,128)(2,1)S(1)}, u32[]{:S(2)}, u32[]{:S(2)}) %collective-permute-start.12) | collective-permute-done | bytes 928 | tf_op jit(solution)/shard_map/ppermute | solution.py:21
  92.5 10.3 %collective-permute-done.10 = bf16[1,192,2048]{2,1,0:T(8,128)(2,1)S(1)} collective-permute-done((bf16[1,192,2048]{2,1,0:T(8,128)(2,1)S(1)}, bf16[1,192,2048]{2,1,0:T(8,128)(2,1)S(1)}, u32[]{:S(2)}, u32[]{:S(2)}) %collective-permute-start.10) | collective-permute-done | bytes 786464 | tf_op jit(solution)/shard_map/ppermute | solution.py:21
  120.0 4.1 pad_maximum_fusion
  124.1 3.6 pad_maximum_fusion.1
  143.4 6.1 %fusion.87 = f32[1024,1024]{0,1:T(8,128)} fusion(bf16[1024,2048]{1,0:T(8,128)(2,1)S(1)} %bitcast.247, bf16[1024,2048]{1,0:T(8,128)(2,1)S(1)} %bitcast.256), kind=kOutput, calls=%fused_computation.233 | convolution fusion | flops 4294967296 | bytes 12582912 | tf_op jit(solution)/shard_map/dot_general | solution.py:29
  149.5 11.8 %all-gather.7.cloned.1.call-done = bf16[1024,2048]{1,0:T(8,128)(2,1)} async-done(((bf16[128,2048]{1,0:T(8,128)(2,1)}), bf16[1024,2048]{1,0:T(8,128)(2,1)}) %all-gather.7.cloned.1.call-update) | async-done | bytes 4194320 | tf_op jit(solution)/shard_map/all_gather | solution.py:397
  161.4 12.8 %convert_reduce_fusion = (f32[1024]{0:T(1024)S(1)}, bf16[1024,1024]{0,1:T(8,128)(2,1)}, bf16[1024,1024]{0,1:T(8,128)(2,1)}) fusion(f32[1024,1024]{0,1:T(8,128)} %fusion.87, f32[1024]{0:T(1024)S(1)} %bitcast.292, bf16[1024,2048]{1,0:T(8,128)(2,1)} %all-gather.7.cloned.1.call-done, bf16[1024,2048]{1,0:T(8,128)(2,1)} %bitcast.257), kind=kOutput, calls=%fused_computation.25 | convolution fusion | flops 4321180672 | bytes 16785408 | tf_op jit(solution)/shard_map/dot_general | solution.py:29
  174.9 22.5 %attention_forward.1 = (bf16[8,128,64]{2,1,0:T(8,128)(2,1)}, bf16[8,128,64]{2,1,0:T(8,128)(2,1)}, bf16[8,128,64]{2,1,0:T(8,128)(2,1)}, bf16[8,128,64]{2,1,0:T(8,...) custom-call(s32[8]{0:T(128)} %get-tuple-element.109.refs_0_, ...), custom_call_target="tpu_custom_call" | custom-call | flops 20000000000 | bytes 12000000 | tf_op jit(solution)/shard_map/attention_forward/pallas_call | solution.py:302
  199.6 6.4 %fusion.88 = f32[1024,2048]{1,0:T(8,128)S(1)} fusion(bf16[1024,1024]{0,1:T(8,128)(2,1)} %get-tuple-element.53, bf16[1024,2048]{1,0:T(8,128)(2,1)S(1)} %bitcast.258), kind=kOutput, calls=%fused_computation.234 | convolution fusion | flops 4294967296 | bytes 14680064 | tf_op jit(solution)/shard_map/dot_general | solution.py:25
  224.0 10.7 %fusion.89 = f32[1024,2048]{1,0:T(8,128)} fusion(bf16[1024,1024]{0,1:T(8,128)(2,1)} %get-tuple-element.50, bf16[1024,2048]{1,0:T(8,128)(2,1)} %bitcast.255), kind=kOutput, calls=%fused_computation.235 | convolution fusion | flops 4294967296 | bytes 14680064 | tf_op jit(solution)/shard_map/dot_general | solution.py:25
  237.0 25.5 %attention_backward.1 = (bf16[8,128,192]{2,1,0:T(8,128)(2,1)}, bf16[8,128,192]{2,1,0:T(8,128)(2,1)}, bf16[8,128,192]{2,1,0:T(8,128)(2,1)}, bf16[8,128,192]{2,1,0:T(8,128)(2,1)}) custom-call(s32[8]{0:T(128)} %get-tuple-element.109.refs_0_, s32[8]{0:T(128)} %get-tuple-element.110.refs_1_, bf16[8,128,64]{2,1,0:T(8,128)(2,1)} %bitcast.280, ...), custom_call_target="tpu_custom_call" | custom-call | flops 20000000000 | bytes 12000000 | tf_op jit(solution)/shard_map/attention_backward/pallas_call | solution.py:355
  267.9 9.7 %collective-permute-done.29 = bf16[8,128,192]{2,1,0:T(8,128)(2,1)S(1)} collective-permute-done((bf16[8,128,192]{2,1,0:T(8,128)(2,1)}, bf16[8,128,192]{2,1,0:T(8,128)(2,1)S(1)}, u32[]{:S(2)}, u32[]{:S(2)}) %collective-permute-start.29) | collective-permute-done | bytes 393248 | tf_op jit(solution)/shard_map/ppermute | solution.py:21
  277.6 10.4 %collective-permute-done.31 = bf16[8,128,192]{2,1,0:T(8,128)(2,1)S(1)} collective-permute-done((bf16[8,128,192]{2,1,0:T(8,128)(2,1)}, bf16[8,128,192]{2,1,0:T(8,128)(2,1)S(1)}, u32[]{:S(2)}, u32[]{:S(2)}) %collective-permute-start.31) | collective-permute-done | bytes 393248 | tf_op jit(solution)/shard_map/ppermute | solution.py:21
  288.9 7.8 %add_convert_fusion = bf16[1024,2048]{1,0:T(8,128)(2,1)} fusion(f32[1024,2048]{1,0:T(8,128)} %fusion.89, bf16[1024,768]{1,0:T(8,128)(2,1)S(1)} %bitcast.244, bf16[768,2048]{1,0:T(8,128)(2,1)S(1)} %bitcast.259), kind=kOutput, calls=%fused_computation | convolution fusion | flops 3225419776 | bytes 17301504 | tf_op jit(solution)/shard_map/dot_general | solution.py:25
  296.7 6.3 %fusion.15 = bf16[2,256,2048]{2,1,0:T(8,128)(2,1)} fusion(bf16[2,256,1024]{2,1,0:T(8,128)(2,1)} %bitcast.268, bf16[1024,2048]{1,0:T(8,128)(2,1)} %all-gather.7.cloned.1.call-done), kind=kOutput, calls=%fused_computation.31 | convolution fusion | flops 2148532224 | bytes 7340032 | tf_op jit(solution)/shard_map/dot_general | solution.py:33
  305.5 3.7 convolution_convert_fusion
  321.5 3.9 reshape_reshape.22
  337.4 5.1 %collective-permute-done.48 = bf16[1,64,2048]{2,1,0:T(8,128)(2,1)S(1)} collective-permute-done((bf16[1,64,2048]{2,1,0:T(8,128)(2,1)S(1)}, bf16[1,64,2048]{2,1,0:T(8,128)(2,1)S(1)}, u32[]{:S(2)}, u32[]{:S(2)}) %collective-permute-start.48) | collective-permute-done | bytes 262176 | tf_op jit(solution)/shard_map/ppermute | solution.py:21
  343.3 5.4 %convert_add_fusion = f32[2,256,2048]{2,1,0:T(8,128)S(1)} fusion(bf16[2,256,2048]{2,1,0:T(8,128)(2,1)} %collective-permute-done.51, bf16[2,256,1024]{2,1,0:T(8,128)(2,1)S(1)} %bitcast.267, bf16[1024,2048]{1,0:T(8,128)(2,1)} %all-gather.7.cloned.1.call-done), kind=kOutput, calls=%fused_computation.23 | convolution fusion | flops 2149580800 | bytes 11534336 | tf_op jit(solution)/shard_map/dot_general | solution.py:33
  350.0 4.0 convert_add_fusion.1
  359.8 15.2 %collective-permute-done.52 = bf16[1,256,2048]{2,1,0:T(8,128)(2,1)S(1)} collective-permute-done((bf16[1,256,2048]{2,1,0:T(8,128)(2,1)S(1)}, bf16[1,256,2048]{2,1,0:T(8,128)(2,1)S(1)}, u32[]{:S(2)}, u32[]{:S(2)}) %collective-permute-start.52) | collective-permute-done | bytes 1048608 | tf_op jit(solution)/shard_map/ppermute | solution.py:21
  376.7 20.9 %collective-permute-done.50 = bf16[1,256,2048]{2,1,0:T(8,128)(2,1)S(1)} collective-permute-done((bf16[1,256,2048]{2,1,0:T(8,128)(2,1)S(1)}, bf16[1,256,2048]{2,1,0:T(8,128)(2,1)S(1)}, u32[]{:S(2)}, u32[]{:S(2)}) %collective-permute-start.50) | collective-permute-done | bytes 1048608 | tf_op jit(solution)/shard_map/ppermute | solution.py:21
  399.1 13.9 %collective-permute-done.43 = bf16[1,192,2048]{2,1,0:T(8,128)(2,1)S(1)} collective-permute-done((bf16[1,192,2048]{2,1,0:T(8,128)(2,1)S(1)}, bf16[1,192,2048]{2,1,0:T(8,128)(2,1)S(1)}, u32[]{:S(2)}, u32[]{:S(2)}) %collective-permute-start.43) | collective-permute-done | bytes 786464 | tf_op jit(solution)/shard_map/ppermute | solution.py:21
  (339 shorter events, 164.1 us)
Async XLA Ops:
  7.2 120.4 %all-gather.5.cloned.1.call-start = ((), (), s32[]{:S(2)}) async-start(), calls=%async_computation.4 | async-start | bytes 4718592 | tf_op jit(solution)/shard_map/all_gather | solution.py:397
  10.3 151.1 %all-gather.7.cloned.1.call-start = ((), (), s32[]{:S(2)}) async-start(), calls=%async_computation.5 | async-start | bytes 4718592 | tf_op jit(solution)/shard_map/all_gather | solution.py:397
  11.1 22.5 %collective-permute-start = (bf16[4,64]{1,0:T(4,128)(2,1)S(1)}, bf16[4,64]{1,0:T(4,128)(2,1)S(1)}, u32[]{:S(2)}, u32[]{:S(2)}) collective-permute-start(bf16[4,64]{1,0:T(4,128)(2,1)S(1)} %get-tuple-element.52), channel_id=1, source_target_pairs={{0,1},{1,0},{2,3},{3,2},{4,5},{5,4},{6,7},{7,6},{8,9},{9,8},{10,11... | collective-permute-start | bytes 1544 | tf_op jit(solution)/shard_map/ppermute | solution.py:21
  14.1 23.0 %collective-permute-start.1 = (bf16[4,64]{1,0:T(4,128)(2,1)S(1)}, bf16[4,64]{1,0:T(4,128)(2,1)S(1)}, u32[]{:S(2)}, u32[]{:S(2)}) collective-permute-start(bf16[4,64]{1,0:T(4,128)(2,1)S(1)} %get-tuple-element.52), channel_id=1, source_target_pairs={{0,2},{1,3},{2,0},{3,1},{4,6},{5,7},{6,4},{7,5},{8,10},{9,11},{10,... | collective-permute-start | bytes 1544 | tf_op jit(solution)/shard_map/ppermute | solution.py:21
  15.7 21.5 %collective-permute-start.2 = (bf16[4,64]{1,0:T(4,128)(2,1)S(1)}, bf16[4,64]{1,0:T(4,128)(2,1)S(1)}, u32[]{:S(2)}, u32[]{:S(2)}) collective-permute-start(bf16[4,64]{1,0:T(4,128)(2,1)S(1)} %get-tuple-element.52), channel_id=1, source_target_pairs={{0,3},{1,2},{2,1},{3,0},{4,7},{5,6},{6,5},{7,4},{8,11},{9,10},{10,... | collective-permute-start | bytes 1544 | tf_op jit(solution)/shard_map/ppermute | solution.py:21
  15.7 23.1 %collective-permute-start.3 = (bf16[4,64]{1,0:T(4,128)(2,1)S(1)}, bf16[4,64]{1,0:T(4,128)(2,1)S(1)}, u32[]{:S(2)}, u32[]{:S(2)}) collective-permute-start(bf16[4,64]{1,0:T(4,128)(2,1)S(1)} %get-tuple-element.52), channel_id=1, source_target_pairs={{0,4},{1,5},{2,6},{3,7},{4,0},{5,1},{6,2},{7,3},{8,12},{9,13},{10,... | collective-permute-start | bytes 1544 | tf_op jit(solution)/shard_map/ppermute | solution.py:21
  21.1 393.2 %reduce-scatter.3.cloned.1.call-start = ((), (), s32[]{:S(2)}) async-start(), calls=%async_computation.2 | async-start | bytes 4718592 | tf_op jit(solution)/shard_map/reduce_scatter | solution.py:410
  37.1 50.5 %collective-permute-start.6 = (bf16[4,64]{1,0:T(4,128)(2,1)S(1)}, bf16[4,64]{1,0:T(4,128)(2,1)S(1)}, u32[]{:S(2)}, u32[]{:S(2)}) collective-permute-start(bf16[4,64]{1,0:T(4,128)(2,1)S(1)} %get-tuple-element.52), channel_id=1, source_target_pairs={{0,7},{1,6},{2,5},{3,4},{4,3},{5,2},{6,1},{7,0},{8,15},{9,14},{10,... | collective-permute-start | bytes 1544 | tf_op jit(solution)/shard_map/ppermute | solution.py:21
  37.2 51.9 %collective-permute-start.22 = (bf16[1,256,2048]{2,1,0:T(8,128)(2,1)}, bf16[1,256,2048]{2,1,0:T(8,128)(2,1)S(1)}, u32[]{:S(2)}, u32[]{:S(2)}) collective-permute-start(bf16[1,256,2048]{2,1,0:T(8,128)(2,1)} %bitcast.44), channel_id=1, source_target_pairs={{0,16},{1,17},{2,18},{3,19},{4,20},{5,21},{6,22},{7,23},{8,24},{9,... | collective-permute-start | bytes 3145736 | tf_op jit(solution)/shard_map/ppermute | solution.py:21
  38.8 65.4 %collective-permute-start.24 = (bf16[1,256,2048]{2,1,0:T(8,128)(2,1)}, bf16[1,256,2048]{2,1,0:T(8,128)(2,1)S(1)}, u32[]{:S(2)}, u32[]{:S(2)}) collective-permute-start(bf16[1,256,2048]{2,1,0:T(8,128)(2,1)} %bitcast.46), channel_id=1, source_target_pairs={{0,16},{1,17},{2,18},{3,19},{4,20},{5,21},{6,22},{7,23},{8,24},{9,... | collective-permute-start | bytes 3145736 | tf_op jit(solution)/shard_map/ppermute | solution.py:21
  39.3 46.8 %collective-permute-start.12 = (bf16[1,448]{1,0:T(2,128)(2,1)S(1)}, bf16[1,448]{1,0:T(2,128)(2,1)S(1)}, u32[]{:S(2)}, u32[]{:S(2)}) collective-permute-start(bf16[1,448]{1,0:T(2,128)(2,1)S(1)} %broadcast_in_dim.110), channel_id=1, source_target_pairs={{0,16},{1,17},{2,18},{3,19},{4,20},{5,21},{6,22},{7,23},{8,24},{9,... | collective-permute-start | bytes 2696 | tf_op jit(solution)/shard_map/ppermute | solution.py:21
  40.9 62.0 %collective-permute-start.10 = (bf16[1,192,2048]{2,1,0:T(8,128)(2,1)S(1)}, bf16[1,192,2048]{2,1,0:T(8,128)(2,1)S(1)}, u32[]{:S(2)}, u32[]{:S(2)}) collective-permute-start(bf16[1,192,2048]{2,1,0:T(8,128)(2,1)S(1)} %bitcast.239), channel_id=1, source_target_pairs={{0,16},{1,17},{2,18},{3,19},{4,20},{5,21},{6,22},{7,23},{8,24},{9,... | collective-permute-start | bytes 2359304 | tf_op jit(solution)/shard_map/ppermute | solution.py:21
  86.1 23.6 %collective-permute-start.20 = (bf16[1,64,2048]{2,1,0:T(8,128)(2,1)S(1)}, bf16[1,64,2048]{2,1,0:T(8,128)(2,1)}, u32[]{:S(2)}, u32[]{:S(2)}) collective-permute-start(bf16[1,64,2048]{2,1,0:T(8,128)(2,1)S(1)} %bitcast.270), channel_id=1, source_target_pairs={{0,16},{1,17},{2,18},{3,19},{4,20},{5,21},{6,22},{7,23},{8,24},{9,... | collective-permute-start | bytes 786440 | tf_op jit(solution)/shard_map/ppermute | solution.py:21
  92.2 27.8 %collective-permute-start.23 = (bf16[2,256,2048]{2,1,0:T(8,128)(2,1)}, bf16[2,256,2048]{2,1,0:T(8,128)(2,1)}, u32[]{:S(2)}, u32[]{:S(2)}) collective-permute-start(bf16[2,256,2048]{2,1,0:T(8,128)(2,1)} %pad_maximum_fusion.3), channel_id=1, source_target_pairs={{0,8},{1,9},{2,10},{3,11},{4,12},{5,13},{6,14},{7,15},{8,0},{9,1},... | collective-permute-start | bytes 6291464 | tf_op jit(solution)/shard_map/ppermute | solution.py:21
  141.3 32.8 %collective-permute-start.14 = (bf16[8,128,192]{2,1,0:T(8,128)(2,1)S(1)}, bf16[8,128,192]{2,1,0:T(8,128)(2,1)S(1)}, u32[]{:S(2)}, u32[]{:S(2)}) collective-permute-start(bf16[8,128,192]{2,1,0:T(8,128)(2,1)S(1)} %bitcast.278), channel_id=1, source_target_pairs={{0,16},{1,17},{2,18},{3,19},{4,20},{5,21},{6,22},{7,23},{8,24},{9,... | collective-permute-start | bytes 1179656 | tf_op jit(solution)/shard_map/ppermute | solution.py:21
  142.6 31.5 %collective-permute-start.15 = (bf16[8,128,192]{2,1,0:T(8,128)(2,1)S(1)}, bf16[8,128,192]{2,1,0:T(8,128)(2,1)}, u32[]{:S(2)}, u32[]{:S(2)}) collective-permute-start(bf16[8,128,192]{2,1,0:T(8,128)(2,1)S(1)} %bitcast.277), channel_id=1, source_target_pairs={{0,8},{1,9},{2,10},{3,11},{4,12},{5,13},{6,14},{7,15},{8,0},{9,1},... | collective-permute-start | bytes 1179656 | tf_op jit(solution)/shard_map/ppermute | solution.py:21
  142.6 31.5 %collective-permute-start.16 = (bf16[8,128,192]{2,1,0:T(8,128)(2,1)S(1)}, bf16[8,128,192]{2,1,0:T(8,128)(2,1)}, u32[]{:S(2)}, u32[]{:S(2)}) collective-permute-start(bf16[8,128,192]{2,1,0:T(8,128)(2,1)S(1)} %bitcast.276), channel_id=1, source_target_pairs={{0,24},{1,25},{2,26},{3,27},{4,28},{5,29},{6,30},{7,31},{8,16},{9,... | collective-permute-start | bytes 1179656 | tf_op jit(solution)/shard_map/ppermute | solution.py:21
  213.0 203.5 %reduce-scatter.5.cloned.1.call-start = ((), (), s32[]{:S(2)}) async-start(), calls=%async_computation.3 | async-start | bytes 4718592 | tf_op jit(solution)/shard_map/reduce_scatter | solution.py:410
  264.3 23.7 %collective-permute-start.31 = (bf16[8,128,192]{2,1,0:T(8,128)(2,1)}, bf16[8,128,192]{2,1,0:T(8,128)(2,1)S(1)}, u32[]{:S(2)}, u32[]{:S(2)}) collective-permute-start(bf16[8,128,192]{2,1,0:T(8,128)(2,1)} %get-tuple-element.41), channel_id=1, source_target_pairs={{0,24},{1,25},{2,26},{3,27},{4,28},{5,29},{6,30},{7,31},{8,16},{9,... | collective-permute-start | bytes 1179656 | tf_op jit(solution)/shard_map/ppermute | solution.py:21
  303.1 40.2 %collective-permute-start.51 = (bf16[2,256,2048]{2,1,0:T(8,128)(2,1)}, bf16[2,256,2048]{2,1,0:T(8,128)(2,1)}, u32[]{:S(2)}, u32[]{:S(2)}) collective-permute-start(bf16[2,256,2048]{2,1,0:T(8,128)(2,1)} %fusion.15), channel_id=1, source_target_pairs={{0,8},{1,9},{2,10},{3,11},{4,12},{5,13},{6,14},{7,15},{8,0},{9,1},... | collective-permute-start | bytes 6291464 | tf_op jit(solution)/shard_map/ppermute | solution.py:21
  309.1 40.9 %collective-permute-start.49 = (bf16[2,256,2048]{2,1,0:T(8,128)(2,1)}, bf16[2,256,2048]{2,1,0:T(8,128)(2,1)}, u32[]{:S(2)}, u32[]{:S(2)}) collective-permute-start(bf16[2,256,2048]{2,1,0:T(8,128)(2,1)} %convolution_convert_fusion), channel_id=1, source_target_pairs={{0,8},{1,9},{2,10},{3,11},{4,12},{5,13},{6,14},{7,15},{8,0},{9,1},... | collective-permute-start | bytes 6291464 | tf_op jit(solution)/shard_map/ppermute | solution.py:21
  348.9 26.1 %collective-permute-start.52 = (bf16[1,256,2048]{2,1,0:T(8,128)(2,1)S(1)}, bf16[1,256,2048]{2,1,0:T(8,128)(2,1)S(1)}, u32[]{:S(2)}, u32[]{:S(2)}) collective-permute-start(bf16[1,256,2048]{2,1,0:T(8,128)(2,1)S(1)} %slice.401), channel_id=1, source_target_pairs={{0,16},{1,17},{2,18},{3,19},{4,20},{5,21},{6,22},{7,23},{8,24},{9,... | collective-permute-start | bytes 3145736 | tf_op jit(solution)/shard_map/ppermute | solution.py:21
  354.2 43.3 %collective-permute-start.50 = (bf16[1,256,2048]{2,1,0:T(8,128)(2,1)S(1)}, bf16[1,256,2048]{2,1,0:T(8,128)(2,1)S(1)}, u32[]{:S(2)}, u32[]{:S(2)}) collective-permute-start(bf16[1,256,2048]{2,1,0:T(8,128)(2,1)S(1)} %slice.402), channel_id=1, source_target_pairs={{0,16},{1,17},{2,18},{3,19},{4,20},{5,21},{6,22},{7,23},{8,24},{9,... | collective-permute-start | bytes 3145736 | tf_op jit(solution)/shard_map/ppermute | solution.py:21
  358.7 54.3 %collective-permute-start.43 = (bf16[1,192,2048]{2,1,0:T(8,128)(2,1)S(1)}, bf16[1,192,2048]{2,1,0:T(8,128)(2,1)S(1)}, u32[]{:S(2)}, u32[]{:S(2)}) collective-permute-start(bf16[1,192,2048]{2,1,0:T(8,128)(2,1)S(1)} %slice.403), channel_id=1, source_target_pairs={{0,16},{1,17},{2,18},{3,19},{4,20},{5,21},{6,22},{7,23},{8,24},{9,... | collective-permute-start | bytes 2359304 | tf_op jit(solution)/shard_map/ppermute | solution.py:21
  (75 other events, 894.4 us)
Sparse Core Ops, SparseCore 0:
  10.7 76.1 all-gather.4
  89.7 71.6 all-gather.6
  213.1 88.0 reduce-scatter.2
  305.2 87.6 reduce-scatter.4
